TPU v7x, 256 devices: a whole 4x4x8 slice. The times are simulated.
256 devices in a mesh: rep: 16 (over z_hi, x), fsdp: 16 (over z_lo, y, core).
Axes of the slice: x: 4, y: 4, z: 8 (z_hi: 4, z_lo: 2; z = z_hi * 2 + z_lo), core: 2. Of those that a mesh axis runs over, the one named last changes fastest.
Arguments:
- anchor: float32 [16, 128, 25600], P('rep', 'fsdp'), may hold values from -6 to 6
- momentum: float32 [16, 128, 25600], P('rep', 'fsdp'), may hold values from -4 to 4
- adam_first: float32 [16, 128, 25600], P('rep', 'fsdp'), may hold values from -4 to 4
- adam_second: float32 [16, 128, 25600], P('rep', 'fsdp'), may hold values from 0.05 to 2
- gradients: bfloat16 [2, 16, 128, 25600], P(None, 'rep', 'fsdp'), may hold values from -6 to 6
- probe_tokens: bfloat16 [2, 16, 1024, 128], P(None, 'rep', 'fsdp'), may hold values from -0.52734375 to 0.52734375
- matching: int32 [2, 16], replicated, may hold values from 0 to 15, as said below
Outputs:
- anchor_out: float32 [16, 128, 25600], P('rep', 'fsdp')
- momentum_out: float32 [16, 128, 25600], P('rep', 'fsdp')
- evaluated: bfloat16 [2, 16, 1024, 25600], P(None, 'rep', 'fsdp')
Inputs may be any that keep to these rules, and one draw needn't show every extreme that they name: In each outer step the matching pairs the replicas: matching[s, matching[s, r]] = r and matching[s, r] != r.
All inputs are finite; a program needn't handle non-finite values.
Results may differ from a plain program's by a relative error of at most 0.0049.
Values may be sent and summed in bfloat16 or wider, within the bound.
No kernel may reach another device: no remote copies, remote signals or barrier semaphores. Data moves between devices by JAX's collectives and lax.ppermute only.
A program may use at most 128 MiB of HBM per device.

v0:
```python
import jax
import jax.numpy as jnp
from jax import lax
from jax.sharding import PartitionSpec as P

INNER = 4


first_decay = 0.9
second_decay = 0.95
inner_rate = 0.2
weight_decay = 0.1
outer_rate = 0.7
outer_beta = 0.9
epsilon = 1e-08


def reorder(received, partners, replicas):
    blocks = received.reshape(replicas, received.shape[0] // replicas, received.shape[1])
    return jnp.take(blocks, partners, axis=0).reshape(received.shape)


def relay_pair(anchor_rows, momentum_rows, partners):
    replicas = lax.axis_size("rep")
    spread = (
        lax.all_to_all(anchor_rows, "rep", split_axis=1, concat_axis=0, tiled=True),
        lax.all_to_all(momentum_rows, "rep", split_axis=1, concat_axis=0, tiled=True),
    )
    first_sorted = reorder(spread[0], partners, replicas)
    second_sorted = reorder(spread[1], partners, replicas)
    return (
        lax.all_to_all(first_sorted, "rep", split_axis=0, concat_axis=1, tiled=True),
        lax.all_to_all(second_sorted, "rep", split_axis=0, concat_axis=1, tiled=True),
    )


def shards(anchor, momentum, adam_first, adam_second, gradients, probe_tokens, matching):
    anchor_rows = anchor[0]
    momentum_rows = momentum[0]
    first_moment = adam_first[0]
    second_moment = adam_second[0]
    evaluations = []
    for outer_step in range(gradients.shape[0]):
        partners = matching[outer_step]
        partner_anchor, partner_momentum = relay_pair(anchor_rows, momentum_rows, partners)
        carried = 0.5 * (momentum_rows + partner_momentum)
        mixed = 0.5 * (anchor_rows + partner_anchor)
        gradient = gradients[outer_step, 0].astype(jnp.float32)
        inner_weights = mixed
        for inner_pass in range(INNER):
            first_moment = first_decay * first_moment + (1.0 - first_decay) * gradient
            second_moment = (
                second_decay * second_moment + (1.0 - second_decay) * gradient * gradient
            )
            inner_weights = inner_weights - inner_rate * (
                first_moment / (jnp.sqrt(second_moment) + epsilon) + weight_decay * inner_weights
            )
        momentum_rows = outer_beta * carried + (mixed - inner_weights)
        anchor_rows = mixed - outer_rate * momentum_rows
        weights = anchor_rows.astype(jnp.bfloat16)
        tokens = probe_tokens[outer_step, 0]
        running_sum = jnp.dot(
            tokens,
            lax.all_gather(weights, "fsdp", axis=0, tiled=True),
            preferred_element_type=jnp.float32,
        )
        evaluated = running_sum.astype(jnp.bfloat16)
        evaluations.append(evaluated)
    return (anchor_rows[None], momentum_rows[None], jnp.stack(evaluations)[:, None])


def solution(mesh):
    placed = (
        P("rep", "fsdp", None),
        P("rep", "fsdp", None),
        P("rep", "fsdp", None),
        P("rep", "fsdp", None),
        P(None, "rep", "fsdp", None),
        P(None, "rep", "fsdp", None),
        P(),
    )
    return jax.shard_map(
        shards,
        mesh=mesh,
        in_specs=placed,
        out_specs=(P("rep", "fsdp", None), P("rep", "fsdp", None), P(None, "rep", "fsdp", None)),
        check_vma=False,
    )
```

profile of v0, /device:TPU:1, one launch (start us, length us, event | category | flops | bytes accessed | tf_op | source)
XLA Modules:
  0.0 350.8 jit_solution(17773876855095156924)
XLA Ops:
  9.8 11.6 %all-to-all-start.2 = ((f32[8,16,1600]{2,0,1:T(8,128)}), f32[8,16,1600]{2,0,1:T(8,128)S(1)}, u32[]{:S(2)}, u32[]{:S(2)}) async-start(f32[8,16,1600]{2,0,1:T(8,128)} %copy.14), calls=%async_computation.2 | async-start | bytes 1703936 | tf_op jit(solution)/shard_map/all_to_all | solution.py:27
  24.1 18.2 %all-to-all-done.2 = f32[8,16,1600]{2,0,1:T(8,128)S(1)} async-done(((f32[8,16,1600]{2,0,1:T(8,128)}), f32[8,16,1600]{2,0,1:T(8,128)S(1)}, u32[]{:S(2)}, u32[]{:S(2)}) %all-to-all-start.2) | async-done | bytes 819232 | tf_op jit(solution)/shard_map/all_to_all | solution.py:27
  42.3 7.8 %all-to-all-start = ((f32[8,16,1600]{2,0,1:T(8,128)}), f32[8,16,1600]{2,0,1:T(8,128)}, u32[]{:S(2)}, u32[]{:S(2)}) async-start(f32[8,16,1600]{2,0,1:T(8,128)} %copy.12), calls=%async_computation | async-start | bytes 1703936 | tf_op jit(solution)/shard_map/all_to_all | solution.py:26
  51.6 19.1 %all-to-all-done = f32[8,16,1600]{2,0,1:T(8,128)} async-done(((f32[8,16,1600]{2,0,1:T(8,128)}), f32[8,16,1600]{2,0,1:T(8,128)}, u32[]{:S(2)}, u32[]{:S(2)}) %all-to-all-start) | async-done | bytes 819232 | tf_op jit(solution)/shard_map/all_to_all | solution.py:26
  74.7 25.0 %all_to_all.134 = f32[16,8,1600]{2,1,0:T(8,128)} all-to-all(f32[16,8,1600]{2,1,0:T(8,128)S(1)} %get-tuple-element.31), channel_id=1, replica_groups=mesh['rep'=16,'fsdp'=16] {'rep'}, dimensions={0} | all-to-all | bytes 1638400 | tf_op jit(solution)/shard_map/all_to_all | solution.py:32
  99.7 5.1 %all-to-all-start.3 = ((f32[16,8,1600]{2,1,0:T(8,128)}), f32[16,8,1600]{2,1,0:T(8,128)}, u32[]{:S(2)}, u32[]{:S(2)}) async-start(f32[16,8,1600]{2,1,0:T(8,128)} %get-tuple-element.30), calls=%async_computation.3 | async-start | bytes 1703936 | tf_op jit(solution)/shard_map/all_to_all | solution.py:33
  105.8 2.4 reshape.136
  112.9 2.4 all_to_all.122
  115.3 3.2 all-to-all-done.3
  123.0 2.4 all_to_all.123
  125.5 5.1 %subtract_add_fusion.2 = (f32[1,8,25600]{2,1,0:T(8,128)}, f32[1,8,25600]{2,1,0:T(8,128)}, f32[1,8,25600]{2,1,0:T(8,128)}) fusion(f32[1,8,25600]{2,1,0:T(8,128)} %param.10, f32[1,8,25600]{2,1,0:T(8,128)} %all_to_all.111, f32[1,8,25600]{2,1,0:T(8,128)S(1)} %copy-done, f32[1,8,25600]{2,1,0:T(8,128)} %all_to_all.105, bf16[2,1,8,25600]{3,2,1,0:T(8,128)(2,1)S(1)} %copy-done.3, ...), kind=kLoop, calls=%fused_computation.80 | loop fusion | flops 10240000 | bytes 7782400 | tf_op jit(solution)/shard_map/add | solution.py:58
  135.3 6.6 %multiply_subtract_fusion = (f32[8,16,1600]{2,0,1:T(8,128)}, f32[8,16,1600]{2,0,1:T(8,128)}) fusion(f32[16,8,1600]{2,1,0:T(8,128)} %all_to_all.134, f32[8,16,1600]{2,1,0:T(8,128)} %copy-done.5, f32[8,16,1600]{2,1,0:T(8,128)} %mul.488, f32[8,16,1600]{2,1,0:T(8,128)} %reshape.136, f32[8,16,1600]{2,1,0:T(8,128)} %mul.486, f32[16,8,1600]{2,1,0:T(8,128)} %all-to-all-done.3, ...), kind=kLoop, calls=%fused_computation.36 | loop fusion | flops 10035200 | bytes 7372800 | tf_op jit(solution)/shard_map/sub | solution.py:59
  141.8 5.9 %all-to-all-start.6 = ((f32[8,16,1600]{2,0,1:T(8,128)}), f32[8,16,1600]{2,0,1:T(8,128)}, u32[]{:S(2)}, u32[]{:S(2)}) async-start(f32[8,16,1600]{2,0,1:T(8,128)} %get-tuple-element.18), calls=%async_computation.6 | async-start | bytes 1703936 | tf_op jit(solution)/shard_map/all_to_all | solution.py:27
  147.9 4.9 %fusion.52 = (bf16[8,25600]{1,0:T(8,128)(2,1)}, f32[8,25600]{1,0:T(8,128)}) fusion(f32[8,25600]{1,0:T(8,128)} %all_to_all.122, f32[1,8,25600]{2,1,0:T(8,128)S(1)} %copy-done, f32[1,8,25600]{2,1,0:T(8,128)S(1)} %copy-done.2, bf16[2,1,8,25600]{3,2,1,0:T(8,128)(2,1)S(1)} %copy-done.3, f32[1,8,25600]{2,1,0:T(8,128)S(1)} %copy-done.1, ...), kind=kLoop, calls=%fused_computation.81 | loop fusion | flops 10854400 | bytes 6553600 | tf_op jit(solution)/shard_map/convert_element_type | solution.py:60
  152.9 8.2 %all-to-all-done.6 = f32[8,16,1600]{2,0,1:T(8,128)} async-done(((f32[8,16,1600]{2,0,1:T(8,128)}), f32[8,16,1600]{2,0,1:T(8,128)}, u32[]{:S(2)}, u32[]{:S(2)}) %all-to-all-start.6) | async-done | bytes 819232 | tf_op jit(solution)/shard_map/all_to_all | solution.py:27
  161.1 4.3 %all-to-all-start.4 = ((f32[8,16,1600]{2,0,1:T(8,128)}), f32[8,16,1600]{2,0,1:T(8,128)}, u32[]{:S(2)}, u32[]{:S(2)}) async-start(f32[8,16,1600]{2,0,1:T(8,128)} %get-tuple-element.17), calls=%async_computation.4 | async-start | bytes 1703936 | tf_op jit(solution)/shard_map/all_to_all | solution.py:26
  165.4 2.7 gather_fusion.3
  168.1 19.6 %all-to-all-done.4 = f32[8,16,1600]{2,0,1:T(8,128)} async-done(((f32[8,16,1600]{2,0,1:T(8,128)}), f32[8,16,1600]{2,0,1:T(8,128)}, u32[]{:S(2)}, u32[]{:S(2)}) %all-to-all-start.4) | async-done | bytes 819232 | tf_op jit(solution)/shard_map/all_to_all | solution.py:26
  187.7 2.7 gather_fusion.2
  190.4 2.5 broadcast_select_fusion
  192.9 32.3 %all_to_all.135 = f32[16,8,1600]{2,1,0:T(8,128)} all-to-all(f32[16,8,1600]{2,1,0:T(8,128)S(1)} %get-tuple-element.29), channel_id=1, replica_groups=mesh['rep'=16,'fsdp'=16] {'rep'}, dimensions={0} | all-to-all | bytes 1638400 | tf_op jit(solution)/shard_map/all_to_all | solution.py:32
  225.2 4.3 %all-to-all-start.7 = ((f32[16,8,1600]{2,1,0:T(8,128)}), f32[16,8,1600]{2,1,0:T(8,128)}, u32[]{:S(2)}, u32[]{:S(2)}) async-start(f32[16,8,1600]{2,1,0:T(8,128)} %get-tuple-element.28), calls=%async_computation.7 | async-start | bytes 1703936 | tf_op jit(solution)/shard_map/all_to_all | solution.py:33
  231.8 23.2 %all-to-all-done.7 = f32[16,8,1600]{2,1,0:T(8,128)} async-done(((f32[16,8,1600]{2,1,0:T(8,128)}), f32[16,8,1600]{2,1,0:T(8,128)}, u32[]{:S(2)}, u32[]{:S(2)}) %all-to-all-start.7) | async-done | bytes 819232 | tf_op jit(solution)/shard_map/all_to_all | solution.py:33
  259.6 2.4 all_to_all.124
  262.0 5.0 %subtract_convert_fusion = bf16[8,25600]{1,0:T(8,128)(2,1)} fusion(f32[8,25600]{1,0:T(8,128)} %get-tuple-element.14, f32[8,25600]{1,0:T(8,128)} %all_to_all.125, f32[8,25600]{1,0:T(8,128)} %all_to_all.124, bf16[2,1,8,25600]{3,2,1,0:T(8,128)(2,1)S(1)} %copy-done.3, f32[8,25600]{1,0:T(8,128)} %all_to_all.122, f32[1,8,25600]{2,1,0:T(8,128)S(1)} %copy-done, ...), kind=kLoop, calls=%fused_computation.76 | loop fusion | flops 15769600 | bytes 6963200 | tf_op jit(solution)/shard_map/convert_element_type | solution.py:60
  267.0 2.4 all_to_all.116
  269.4 2.4 all_to_all.121
  271.8 5.2 %multiply_subtract_fusion.2 = (f32[1,8,25600]{2,1,0:T(8,128)}, f32[1,8,25600]{2,1,0:T(8,128)}) fusion(f32[1,8,25600]{2,1,0:T(8,128)} %all_to_all.116, f32[1,8,25600]{2,1,0:T(8,128)} %get-tuple-element.23, f32[1,8,25600]{2,1,0:T(8,128)S(1)} %copy-done, f32[1,8,25600]{2,1,0:T(8,128)} %all_to_all.105, f32[1,8,25600]{2,1,0:T(8,128)S(1)} %copy-done.2, ...), kind=kLoop, calls=%fused_computation.78 | loop fusion | flops 15564800 | bytes 8192000 | tf_op jit(solution)/shard_map/sub | solution.py:59
  277.0 3.9 %fusion = bf16[1,64,25600]{2,1,0:T(8,128)(2,1)S(1)} fusion(bf16[128,25600]{1,0:T(8,128)(2,1)} %all-gather.3.cloned.1.call-done, bf16[2,1,64,128]{3,2,1,0:T(8,128)(2,1)S(1)} %copy-done.6), kind=kOutput, calls=%fused_computation.6 | convolution fusion | flops 421068800 | bytes 9846784 | tf_op jit(solution)/shard_map/dot_general | solution.py:62
  280.9 55.8 %all-gather.5.cloned.1.call-done = bf16[128,25600]{1,0:T(8,128)(2,1)} async-done(((bf16[8,25600]{1,0:T(8,128)(2,1)}), bf16[128,25600]{1,0:T(8,128)(2,1)}) %all-gather.5.cloned.1.call-update) | async-done | bytes 6553616 | tf_op jit(solution)/shard_map/all_gather | solution.py:64
  336.7 3.9 %fusion.1 = bf16[1,64,25600]{2,1,0:T(8,128)(2,1)S(1)} fusion(bf16[128,25600]{1,0:T(8,128)(2,1)} %all-gather.5.cloned.1.call-done, bf16[2,1,64,128]{3,2,1,0:T(8,128)(2,1)S(1)} %copy-done.6), kind=kOutput, calls=%fused_computation.7 | convolution fusion | flops 421068800 | bytes 9846784 | tf_op jit(solution)/shard_map/dot_general | solution.py:62
  340.6 3.4 maximum_bitcast_fusion
  (41 shorter events, 32.9 us)
Async XLA Ops:
  7.2 42.9 %copy-start.7 = (s32[2,16]{1,0:T(2,128)S(1)}, s32[2,16]{1,0:T(2,128)}, u32[]{:S(2)}) copy-start(s32[2,16]{1,0:T(2,128)} %param.15) | copy-start | bytes 388
  8.6 12.8 %copy-start.4 = (f32[8,16,1600]{2,1,0:T(8,128)}, f32[8,16,1600]{2,1,0:T(8,128)S(1)}, u32[]{:S(2)}) copy-start(f32[8,16,1600]{2,1,0:T(8,128)S(1)} %all_to_all.106) | copy-start | bytes 2457604
  9.8 32.4 %all-to-all-start.2 = ((f32[8,16,1600]{2,0,1:T(8,128)}), f32[8,16,1600]{2,0,1:T(8,128)S(1)}, u32[]{:S(2)}, u32[]{:S(2)}) async-start(f32[8,16,1600]{2,0,1:T(8,128)} %copy.14), calls=%async_computation.2 | async-start | bytes 1703936 | tf_op jit(solution)/shard_map/all_to_all | solution.py:27
  22.9 76.8 %copy-start.5 = (f32[8,16,1600]{2,1,0:T(8,128)}, f32[8,16,1600]{2,1,0:T(8,128)S(1)}, u32[]{:S(2)}) copy-start(f32[8,16,1600]{2,1,0:T(8,128)S(1)} %all_to_all.100) | copy-start | bytes 2457604
  22.9 81.9 %copy-start.3 = (bf16[2,1,8,25600]{3,2,1,0:T(8,128)(2,1)S(1)}, bf16[2,1,8,25600]{3,2,1,0:T(8,128)(2,1)}, u32[]{:S(2)}) copy-start(bf16[2,1,8,25600]{3,2,1,0:T(8,128)(2,1)} %param.13) | copy-start | bytes 2457604
  42.3 28.4 %all-to-all-start = ((f32[8,16,1600]{2,0,1:T(8,128)}), f32[8,16,1600]{2,0,1:T(8,128)}, u32[]{:S(2)}, u32[]{:S(2)}) async-start(f32[8,16,1600]{2,0,1:T(8,128)} %copy.12), calls=%async_computation | async-start | bytes 1703936 | tf_op jit(solution)/shard_map/all_to_all | solution.py:26
  99.7 18.7 %all-to-all-start.3 = ((f32[16,8,1600]{2,1,0:T(8,128)}), f32[16,8,1600]{2,1,0:T(8,128)}, u32[]{:S(2)}, u32[]{:S(2)}) async-start(f32[16,8,1600]{2,1,0:T(8,128)} %get-tuple-element.30), calls=%async_computation.3 | async-start | bytes 1703936 | tf_op jit(solution)/shard_map/all_to_all | solution.py:33
  104.8 20.6 %copy-start = (f32[1,8,25600]{2,1,0:T(8,128)S(1)}, f32[1,8,25600]{2,1,0:T(8,128)}, u32[]{:S(2)}) copy-start(f32[1,8,25600]{2,1,0:T(8,128)} %param.9) | copy-start | bytes 2457604
  104.8 20.6 %copy-start.1 = (f32[1,8,25600]{2,1,0:T(8,128)S(1)}, f32[1,8,25600]{2,1,0:T(8,128)}, u32[]{:S(2)}) copy-start(f32[1,8,25600]{2,1,0:T(8,128)} %param.11) | copy-start | bytes 2457604
  104.8 20.6 %copy-start.2 = (f32[1,8,25600]{2,1,0:T(8,128)S(1)}, f32[1,8,25600]{2,1,0:T(8,128)}, u32[]{:S(2)}) copy-start(f32[1,8,25600]{2,1,0:T(8,128)} %param.12) | copy-start | bytes 2457604
  141.8 19.3 %all-to-all-start.6 = ((f32[8,16,1600]{2,0,1:T(8,128)}), f32[8,16,1600]{2,0,1:T(8,128)}, u32[]{:S(2)}, u32[]{:S(2)}) async-start(f32[8,16,1600]{2,0,1:T(8,128)} %get-tuple-element.18), calls=%async_computation.6 | async-start | bytes 1703936 | tf_op jit(solution)/shard_map/all_to_all | solution.py:27
  147.7 129.3 %all-gather.3.cloned.1.call-start = ((), (), s32[]{:S(2)}) async-start(), calls=%async_computation.8 | async-start | bytes 6963200 | tf_op jit(solution)/shard_map/all_gather | solution.py:64
  161.1 26.6 %all-to-all-start.4 = ((f32[8,16,1600]{2,0,1:T(8,128)}), f32[8,16,1600]{2,0,1:T(8,128)}, u32[]{:S(2)}, u32[]{:S(2)}) async-start(f32[8,16,1600]{2,0,1:T(8,128)} %get-tuple-element.17), calls=%async_computation.4 | async-start | bytes 1703936 | tf_op jit(solution)/shard_map/all_to_all | solution.py:26
  225.2 29.8 %all-to-all-start.7 = ((f32[16,8,1600]{2,1,0:T(8,128)}), f32[16,8,1600]{2,1,0:T(8,128)}, u32[]{:S(2)}, u32[]{:S(2)}) async-start(f32[16,8,1600]{2,1,0:T(8,128)} %get-tuple-element.28), calls=%async_computation.7 | async-start | bytes 1703936 | tf_op jit(solution)/shard_map/all_to_all | solution.py:33
  229.5 107.2 %all-gather.5.cloned.1.call-start = ((), (), s32[]{:S(2)}) async-start(), calls=%async_computation.9 | async-start | bytes 6963200 | tf_op jit(solution)/shard_map/all_gather | solution.py:64
  267.0 10.0 %copy-start.6 = (bf16[2,1,64,128]{3,2,1,0:T(8,128)(2,1)S(1)}, bf16[2,1,64,128]{3,2,1,0:T(8,128)(2,1)}, u32[]{:S(2)}) copy-start(bf16[2,1,64,128]{3,2,1,0:T(8,128)(2,1)} %param.14) | copy-start | bytes 98308
Sparse Core Ops, SparseCore 0:
  153.0 91.6 all-gather.2
  267.1 69.5 all-gather.4
where the time goes:
time: 352 us; the launch traced here: 351 us
  waiting for transfers between devices  147 us (42%)
  blocking collectives  57.4 us (16%)
  local copies, waits for them, and re-layouts  49.3 us (14%)
  starting transfers between devices  39.2 us (11%)
  other arithmetic  35.7 us (10%)
  between operations  14.3 us (4%)
  matrix products  7.73 us (2%)
    all_to_all x2, blocking collectives, relay_pair(): lax.all_to_all(first_sorted, 'rep', split_axis=0, concat_axis=1, tiled=True)  57.4 us
    all_gather x2, waiting for transfers between devices, shards(): lax.all_gather(weights, 'fsdp', axis=0, tiled=True)  55.8 us
    all_to_all x2, waiting for transfers between devices, relay_pair(): lax.all_to_all(anchor_rows, 'rep', split_axis=1, concat_axis=0, tiled=True)  38.7 us
    all_to_all x2, waiting for transfers between devices, relay_pair(): lax.all_to_all(momentum_rows, 'rep', split_axis=1, concat_axis=0, tiled=T...  26.4 us
    all_to_all x2, waiting for transfers between devices, relay_pair(): lax.all_to_all(second_sorted, 'rep', split_axis=0, concat_axis=1, tiled=T...  26.3 us
    all_to_all x2, starting transfers between devices, relay_pair(): lax.all_to_all(momentum_rows, 'rep', split_axis=1, concat_axis=0, tiled=T...  17.5 us
    all_to_all x6, local copies, waits for them, and re-layouts, relay_pair(): lax.all_to_all(first_sorted, 'rep', split_axis=0, concat_axis=1, tiled=True)  14.1 us
    all_to_all x6, local copies, waits for them, and re-layouts, relay_pair(): lax.all_to_all(second_sorted, 'rep', split_axis=0, concat_axis=1, tiled=T...  14.1 us
  transfers between devices with their start and end apart: 8, of which 7 were waited for; matrix products, arithmetic and copies ran while one was open for 11% of the time, Pallas kernels for 0%

commit v1 on v0

v1 whole, which is shorter than its diff:
```python
import functools

import jax
import jax.numpy as jnp
from jax import lax
from jax.experimental import pallas as pl
from jax.experimental.pallas import tpu as pltpu
from jax.sharding import PartitionSpec as P

INNER = 4
first_decay = 0.9
second_decay = 0.95
inner_rate = 0.2
weight_decay = 0.1
outer_rate = 0.7
outer_beta = 0.9
epsilon = 1e-08

SHRINK = 1.0 - inner_rate * weight_decay
KEEP = SHRINK**INNER
Z_OF_W = 1.0 - outer_rate * (1.0 - KEEP)
Z_OF_U = -outer_rate * outer_beta
Y_OF_W = 1.0 - KEEP
Y_OF_U = outer_beta

LANES = 128
SLABS = 8
F32 = jnp.float32
BF16 = jnp.bfloat16
VMEM_LIMIT = 14 * 1024 * 1024
PACK_LIMIT = 58 * 1024 * 1024


def params(limit=VMEM_LIMIT):
    return pltpu.CompilerParams(vmem_limit_bytes=limit)


def cost(flops, moved):
    return pl.CostEstimate(flops=int(flops), bytes_accessed=int(moved), transcendentals=0)


def adam(first, second, gradient):
    moved = (1.0 - first_decay) * gradient
    squared = (1.0 - second_decay) * gradient * gradient
    total = None
    for inner_pass in range(INNER):
        first = first_decay * first + moved
        second = second_decay * second + squared
        step = first / (jnp.sqrt(second) + epsilon)
        total = step if total is None else SHRINK * total + step
    return first, second, inner_rate * total


def windows(columns, window):
    slab = columns // SLABS
    return [start for j in range(SLABS) for start in (j * slab, (j + 1) * slab - window)]


def pack_kernel(*refs):
    sources, (packed_ref, d_out), held, arrived = refs[:5], refs[5:7], refs[7:12], refs[12]
    columns, window = d_out.shape[1], packed_ref.shape[3]
    slab = columns // SLABS
    starts = windows(columns, window)
    copies = []
    for j in range(SLABS):
        lanes = pl.ds(j * slab, slab)
        for i, (source, kept) in enumerate(zip(sources, held)):
            piece = source.at[0, 0, :, lanes] if i == 4 else source.at[0, :, lanes]
            copies.append(pltpu.make_async_copy(piece, kept.at[j], arrived.at[j, i]))
            copies[-1].start()
    for j in range(SLABS):
        lanes = pl.ds(j * slab, slab)
        for copy in copies[5 * j : 5 * j + 5]:
            copy.wait()
        w, u, m, v, g = (kept[j] for kept in held)
        d = adam(m, v, g.astype(F32))[2]
        d_out[:, lanes] = d
        sent = (Z_OF_W * w + Z_OF_U * u, Y_OF_U * u + Y_OF_W * w, d)
        for relay in (2 * j, 2 * j + 1):
            start = starts[relay] - j * slab
            for which, value in enumerate(sent):
                packed_ref[relay, which] = value[:, start : start + window].astype(BF16)


def second_kernel(m_ref, v_ref, g_ref, d_out):
    columns = d_out.shape[1]
    slab = columns // SLABS
    for j in range(SLABS):
        lanes = pl.ds(j * slab, slab)
        first, second = m_ref[0, :, lanes], v_ref[0, :, lanes]
        gradient = g_ref[0, 0, :, lanes].astype(F32)
        for _ in range(INNER):
            first = first_decay * first + (1.0 - first_decay) * gradient
            second = second_decay * second + (1.0 - second_decay) * gradient * gradient
        d_out[:, lanes] = adam(first, second, g_ref[1, 0, :, lanes].astype(F32))[2]


def mean(got_ref, which, r, p):
    return 0.5 * (got_ref[r, which].astype(F32) + got_ref[p, which].astype(F32))


def after_first_step(got_ref, r, p, of_w, of_u):
    shared = mean(got_ref, 0, r, p)
    d = got_ref[r, 2].astype(F32)
    return of_w * (shared - outer_rate * d) + of_u * (mean(got_ref, 1, r, p) + d), shared


def relay_kernel(matching_ref, got_ref, d_ref, tokens_ref, back_ref, held_ref):
    replicas = got_ref.shape[0]

    @pl.loop(0, replicas)
    def _(r):
        held_ref[r], shared = after_first_step(got_ref, r, matching_ref[0, r], Z_OF_W, Z_OF_U)
        back_ref[r, 0] = shared.astype(BF16)

    @pl.loop(0, replicas)
    def _(r):
        back_ref[r, 1] = (0.5 * (held_ref[r] + held_ref[matching_ref[1, r]])).astype(BF16)


def momentum_relay_kernel(matching_ref, got_ref, after_ref, back_ref, held_ref):
    replicas = got_ref.shape[0]

    @pl.loop(0, replicas)
    def _(r):
        held_ref[r] = after_first_step(got_ref, r, matching_ref[0, r], Y_OF_W, Y_OF_U)[0]

    @pl.loop(0, replicas)
    def _(r):
        back_ref[r] = (0.5 * (held_ref[r] + held_ref[matching_ref[1, r]])).astype(BF16)


def joined(first, last, slab):
    overlap = first.shape[1] + last.shape[1] - slab
    return jnp.concatenate([first, last[:, overlap:]], axis=1).astype(F32)


def weights_kernel(core_ref, back_ref, d1_ref, d2_ref, *refs):
    parts, w_ref = refs[:4], refs[4]
    slab = d1_ref.shape[1] // SLABS
    for j in range(SLABS):
        lanes = pl.ds(j * slab, slab)
        first, second = (joined(back_ref[2 * j, i], back_ref[2 * j + 1, i], slab) for i in range(2))
        first = first - outer_rate * d1_ref[:, lanes]
        second = second - outer_rate * d2_ref[:, lanes]
        w_ref[0, :, lanes] = second
        quarter, lanes = j % (SLABS // 2) // 2, pl.ds(j % 2 * slab, slab)
        mine = core_ref[0] == j // (SLABS // 2)
        for away, chosen in enumerate((mine, jnp.logical_not(mine))):
            part = parts[2 * quarter + away]

            @pl.when(chosen)
            def _(part=part, lanes=lanes, first=first, second=second):
                part[0, :, lanes] = first.astype(BF16)
                part[1, :, lanes] = second.astype(BF16)


def momentum_kernel(back_ref, d_ref, u_ref):
    slab = d_ref.shape[1] // SLABS
    for j in range(SLABS):
        lanes = pl.ds(j * slab, slab)
        u_ref[0, :, lanes] = joined(back_ref[2 * j], back_ref[2 * j + 1], slab) + d_ref[:, lanes]


def copy_kernel(from_ref, after_ref, to_ref):
    for step in range(to_ref.shape[0]):
        to_ref[step] = from_ref[step]


def chip_kernel(*refs):
    pieces, out = refs[:4], refs[-1]
    for i, piece in enumerate(pieces):
        for step in range(out.shape[0]):
            out[step, i] = piece[step]


TILES = 5


def evaluate_kernel(quarter, core_ref, tokens_ref, *refs):
    blocks, (out_ref, sent_ref, own_ref, done) = refs[:4], refs[-4:]
    steps, tokens, width = sent_ref.shape
    tile = width // TILES
    start = pl.multiple_of(core_ref[0] * (2 * width) + quarter * width, LANES)
    copies = []
    for step in range(steps):
        for j in range(TILES):
            lanes = pl.ds(j * tile, tile)
            rows = jnp.concatenate([block[step, i, :, lanes] for block in blocks for i in range(4)], axis=0)
            product = jnp.dot(tokens_ref[step], rows, preferred_element_type=F32).astype(BF16)
            own_ref[step, :, lanes] = product[:tokens]
            sent_ref[step, :, lanes] = product[tokens:]
            copies.append(
                pltpu.make_async_copy(
                    own_ref.at[step, :, lanes],
                    out_ref.at[step, 0, :, pl.ds(pl.multiple_of(start + j * tile, LANES), tile)],
                    done.at[step, j],
                )
            )
            copies[-1].start()
    for copy in copies:
        copy.wait()


def place_kernel(quarter, core_ref, piece_ref, buffer_ref, out_ref, done):
    steps, _, width = piece_ref.shape
    tile = width // TILES
    start = pl.multiple_of((1 - core_ref[0]) * (2 * width) + quarter * width, LANES)
    copies = []
    for step in range(steps):
        for j in range(TILES):
            copies.append(
                pltpu.make_async_copy(
                    piece_ref.at[step, :, pl.ds(j * tile, tile)],
                    out_ref.at[step, 0, :, pl.ds(pl.multiple_of(start + j * tile, LANES), tile)],
                    done.at[step, j],
                )
            )
            copies[-1].start()
    for copy in copies:
        copy.wait()


def shards(anchor, momentum, adam_first, adam_second, gradients, probe_tokens, matching):
    replicas = lax.axis_size("rep")
    group = lax.axis_size("fsdp")
    _, rows, columns = anchor.shape
    steps, _, tokens, depth = probe_tokens.shape
    slab = columns // SLABS
    window = LANES * (-(-slab // (2 * LANES)))
    quarter = columns // 4
    unit = rows * columns
    ring = group // 4
    place = lax.axis_index("fsdp")
    core = lax.rem(place, 2).astype(jnp.int32)
    core_ref = core[None]

    whole = pl.BlockSpec(memory_space=pltpu.VMEM)
    scalar = pl.BlockSpec(memory_space=pltpu.SMEM)
    far = pl.BlockSpec(memory_space=pltpu.HBM)
    loose = pl.BlockSpec(memory_space=pl.ANY)
    flat = jax.ShapeDtypeStruct((rows, columns), F32)
    whole_out = jax.ShapeDtypeStruct((1, rows, columns), F32)
    part = jax.ShapeDtypeStruct((steps, rows, quarter), BF16)
    chip = jax.ShapeDtypeStruct((steps, 4, rows, quarter), BF16)
    moved = jax.ShapeDtypeStruct((replicas, 3, rows, window), BF16)
    two_backs = jax.ShapeDtypeStruct((replicas, 2, rows, window), BF16)
    one_back = jax.ShapeDtypeStruct((replicas, rows, window), BF16)
    products = jax.ShapeDtypeStruct((steps, 1, tokens, columns), BF16)
    sent_products = jax.ShapeDtypeStruct((steps, tokens, quarter), BF16)

    def call(kernel, name, in_specs, out_specs, out_shape, flops, nbytes, limit=VMEM_LIMIT, **rest):
        return pl.pallas_call(
            kernel,
            in_specs=in_specs,
            out_specs=out_specs,
            out_shape=out_shape,
            compiler_params=params(limit),
            cost_estimate=cost(flops, nbytes),
            name=name,
            **rest,
        )

    def at(z, y, c):
        return (z * ring + y % ring) * 2 + c

    def permute(value, dz=0, dy=0, dc=0):
        pairs = [
            (at(z, y, c), at(z ^ dz, y + dy, c ^ dc))
            for z in range(2)
            for y in range(ring)
            for c in range(2)
        ]
        return lax.ppermute(value, "fsdp", pairs)

    def relayed(value):
        return lax.all_to_all(value, "rep", 0, 0, tiled=True)

    z_at, y_at = place // (2 * ring), (place // 2) % ring
    owners = jnp.stack(
        [
            ((z_at ^ dz) * ring + (y_at + dy) % ring) * 2 + (core ^ dc)
            for dy in (0, -1, 1, 2)
            for dz in range(2)
            for dc in range(2)
        ]
    )
    own_tokens = probe_tokens[:, 0]
    chip_tokens = jnp.concatenate([own_tokens, permute(own_tokens, dc=1)], axis=1)
    chip_tokens = jnp.take(
        chip_tokens.reshape(steps, 2 * tokens, group, depth // group), owners, axis=2
    ).reshape(steps, 2 * tokens, depth)

    packed, d1 = call(
        pack_kernel,
        "pack",
        [far] * 5,
        [whole] * 2,
        [moved, flat],
        100 * unit,
        26 * unit,
        PACK_LIMIT,
        scratch_shapes=[pltpu.VMEM((SLABS, rows, slab), t) for t in (F32, F32, F32, F32, BF16)]
        + [pltpu.SemaphoreType.DMA((SLABS, 5))],
    )(anchor, momentum, adam_first, adam_second, gradients)
    got = relayed(packed)
    d2 = call(second_kernel, "second", [whole] * 3, whole, flat, 120 * unit, 14 * unit)(
        adam_first, adam_second, gradients
    )

    back = call(
        relay_kernel,
        "relay",
        [scalar, whole, loose, loose],
        whole,
        two_backs,
        30 * unit,
        10 * unit,
        scratch_shapes=[pltpu.VMEM((replicas, rows, window), F32)],
    )(matching, got, d2, chip_tokens)
    kept_low, sent_low, kept_high, sent_high, anchor_out = call(
        weights_kernel,
        "weights",
        [scalar, whole, whole, whole],
        [whole] * 5,
        [part] * 4 + [whole_out],
        8 * unit,
        24 * unit,
    )(core_ref, relayed(back), d1, d2)

    def chip_rows(kept, sent, *after):
        pieces = kept, permute(sent, dc=1), permute(kept, dz=1), permute(sent, dz=1, dc=1)
        return call(
            chip_kernel, "chip", [whole] * 4 + [loose] * len(after), whole, chip, 0, 8 * unit
        )(*pieces, *after)

    low = chip_rows(kept_low, sent_low)
    low_up, low_down = permute(low, dy=1), permute(low, dy=-1)
    low_far = permute(low_up, dy=1)
    high = chip_rows(kept_high, sent_high, low_up, low_down)
    high_down = permute(high, dy=-1)
    later_high = call(copy_kernel, "later", [whole, loose], whole, chip, 0, 8 * unit)(high, low_far)
    high_up = permute(later_high, dy=1)
    high_far = permute(high_down, dy=-1)
    last = call(
        momentum_relay_kernel,
        "momentum_relay",
        [scalar, whole, loose],
        whole,
        one_back,
        30 * unit,
        8 * unit,
        scratch_shapes=[pltpu.VMEM((replicas, rows, window), F32)],
    )(matching, got, later_high)
    momentum_out = call(momentum_kernel, "momentum", [whole] * 2, whole, whole_out, 2 * unit, 10 * unit)(
        relayed(last), d2
    )

    def evaluate(at_quarter, blocks, buffer, *after):
        kernel = functools.partial(evaluate_kernel, at_quarter)
        operands = [core_ref, chip_tokens, *blocks, *after]
        in_specs = [scalar] + [whole] * 5 + [loose] * len(after)
        aliases = {}
        if buffer is not None:
            aliases = {len(operands): 0}
            operands.append(buffer)
            in_specs.append(far)
        return call(
            kernel,
            "evaluate",
            in_specs,
            [far, whole],
            [products, sent_products],
            8 * tokens * depth * quarter,
            16 * unit,
            input_output_aliases=aliases,
            scratch_shapes=[
                pltpu.VMEM((steps, tokens, quarter), BF16),
                pltpu.SemaphoreType.DMA((steps, TILES)),
            ],
        )(*operands)

    def put(at_quarter, piece, buffer):
        return call(
            functools.partial(place_kernel, at_quarter),
            "place",
            [scalar, whole, far],
            far,
            products,
            0,
            8 * unit,
            input_output_aliases={2: 0},
            scratch_shapes=[pltpu.SemaphoreType.DMA((steps, TILES))],
        )(core_ref, piece, buffer)

    buffer, low_sent = evaluate(0, (low, low_up, low_down, low_far), None, later_high)
    buffer, high_sent = evaluate(1, (high, high_up, high_down, high_far), buffer, momentum_out)
    buffer = put(0, permute(low_sent, dc=1), buffer)
    buffer = put(1, permute(high_sent, dc=1), buffer)
    return anchor_out, momentum_out, buffer


def solution(mesh):
    placed = (
        P("rep", "fsdp", None),
        P("rep", "fsdp", None),
        P("rep", "fsdp", None),
        P("rep", "fsdp", None),
        P(None, "rep", "fsdp", None),
        P(None, "rep", "fsdp", None),
        P(),
    )
    return jax.shard_map(
        shards,
        mesh=mesh,
        in_specs=placed,
        out_specs=(P("rep", "fsdp", None), P("rep", "fsdp", None), P(None, "rep", "fsdp", None)),
        check_vma=False,
    )
```

time: 352 us -> 176 us (0.50)
  waiting for transfers between devices: 147 us -> 72 us
  local copies, waits for them, and re-layouts: 49.3 us -> 12.1 us
  other arithmetic: 35.7 us -> 0.12 us
  blocking collectives: 57.4 us -> 31.4 us
  Pallas kernels: 0 us -> 23 us
  between operations: 14.3 us -> 1.04 us
  matrix products: 7.73 us -> 0 us
  starting transfers between devices: 39.2 us -> 35.2 us
    all_to_all x6 -> x2, waiting for transfers between devices: 91.4 us -> 28.1 us  [relayed(): return lax.all_to_all(value, 'rep', 0, 0, tiled=True)]
    all_gather x2 -> x0, waiting for transfers between devices: 55.8 us -> none  [shards(): lax.all_gather(weights, 'fsdp', axis=0, tiled=True)]
    ppermute x0 -> x15, waiting for transfers between devices: none -> 43.9 us  [permute(): return lax.ppermute(value, 'fsdp', pairs)]
    all_to_all x16 -> x0, local copies, waits for them, and re-layouts: 33.4 us -> none  [the longest x6 14.1 us: relay_pair(): lax.all_to_all(first_sorted, 'rep', split_axis=0, concat_axis=1, tiled=True)]
    all_to_all x2 -> x1, blocking collectives: 57.4 us -> 31.4 us  [relayed(): return lax.all_to_all(value, 'rep', 0, 0, tiled=True)]
    pallas_call x0 -> x13, Pallas kernels: none -> 23 us  [the longest x2 6.32 us: evaluate(): call(kernel, 'evaluate', in_specs, [far, whole], [products, sent_products...]
    all_to_all x6 -> x2, starting transfers between devices: 38.9 us -> 17.8 us  [relayed(): return lax.all_to_all(value, 'rep', 0, 0, tiled=True)]
    ppermute x0 -> x15, starting transfers between devices: none -> 17.4 us  [permute(): return lax.ppermute(value, 'fsdp', pairs)]
  transfers between devices with their start and end apart: 8 -> 17, of which waited for: 7 -> 10; matrix products, arithmetic and copies ran while one was open for 11% -> 1% of each run, Pallas kernels for 0% -> 8%
where the time goes in v1:
time: 176 us; the launch traced here: 175 us
  waiting for transfers between devices  72 us (41%)
  starting transfers between devices  35.2 us (20%)
  blocking collectives  31.4 us (18%)
  Pallas kernels  23 us (13%)
  local copies, waits for them, and re-layouts  12.1 us (7%)
    ppermute x15, waiting for transfers between devices, permute(): return lax.ppermute(value, 'fsdp', pairs)  43.9 us
    all_to_all x1, blocking collectives, relayed(): return lax.all_to_all(value, 'rep', 0, 0, tiled=True)  31.4 us
    all_to_all x2, waiting for transfers between devices, relayed(): return lax.all_to_all(value, 'rep', 0, 0, tiled=True)  28.1 us
    all_to_all x2, starting transfers between devices, relayed(): return lax.all_to_all(value, 'rep', 0, 0, tiled=True)  17.8 us
    ppermute x15, starting transfers between devices, permute(): return lax.ppermute(value, 'fsdp', pairs)  17.4 us
    unnamed x35, local copies, waits for them, and re-layouts  11 us
    pallas_call x2, Pallas kernels, evaluate(): call(kernel, 'evaluate', in_specs, [far, whole], [products, sent_products...  6.32 us
    pallas_call x1, Pallas kernels, shards(): call(pack_kernel, 'pack', [far] * 5, [whole] * 2, [moved, flat], 100 * un...  4.76 us
  transfers between devices with their start and end apart: 17, of which 10 were waited for; matrix products, arithmetic and copies ran while one was open for 1% of the time, Pallas kernels for 8%

profile of v1, /device:TPU:1, one launch (start us, length us, event | category | flops | bytes accessed | tf_op | source)
XLA Modules:
  0.0 174.8 jit_solution(14830393794363281160)
XLA Ops:
  0.6 4.8 %pack.1 = (bf16[16,3,8,1664]{3,2,1,0:T(8,128)(2,1)}, f32[8,25600]{1,0:T(8,128)}) custom-call(f32[1,8,25600]{2,1,0:T(8,128)} %refs_0_.1, f32[1,8,25600]{2,1,0:T(8,128)} %refs_1_.1, f32[1,8,25600]{2,1,0:T(8,128)} %m_ref.1, f32[1,8,25600]{2,1,0:T(8,128)} %v_ref.1, bf16[2,1,8,25600]{3,2,1,0:T(8,128)(2,1)} %g_ref.1), custom_call_target="tpu_custom_call" | custom-call | flops 20480000 | bytes 5324800 | tf_op jit(solution)/shard_map/pack/pallas_call | solution.py:294
  5.4 11.7 %all-to-all-start = ((bf16[16,3,8,1664]{3,2,1,0:T(8,128)(2,1)}), bf16[16,3,8,1664]{3,2,1,0:T(8,128)(2,1)S(1)}, u32[]{:S(2)}, u32[]{:S(2)}) async-start(bf16[16,3,8,1664]{3,2,1,0:T(8,128)(2,1)} %get-tuple-element.14), calls=%async_computation | async-start | bytes 2555904 | tf_op jit(solution)/shard_map/all_to_all | solution.py:277
  18.8 1.1 copy-done.3
  19.9 1.1 copy-done.4
  21.1 2.3 %second.1.d_ref.d2_ref = f32[8,25600]{1,0:T(8,128)S(1)} custom-call(f32[1,8,25600]{2,1,0:T(8,128)S(1)} %copy-done.2, f32[1,8,25600]{2,1,0:T(8,128)S(1)} %copy-done.3, bf16[2,1,8,25600]{3,2,1,0:T(8,128)(2,1)S(1)} %copy-done.4), custom_call_target="tpu_custom_call" | custom-call | flops 24576000 | bytes 2867200 | tf_op jit(solution)/shard_map/second/pallas_call | solution.py:307
  24.2 23.1 %all-to-all-done.got_ref = bf16[16,3,8,1664]{3,2,1,0:T(8,128)(2,1)S(1)} async-done(((bf16[16,3,8,1664]{3,2,1,0:T(8,128)(2,1)}), bf16[16,3,8,1664]{3,2,1,0:T(8,128)(2,1)S(1)}, u32[]{:S(2)}, u32[]{:S(2)}) %all-to-all-start) | async-done | bytes 1277984 | tf_op jit(solution)/shard_map/all_to_all | solution.py:277
  47.4 1.3 relay.1
  48.6 31.4 %all_to_all.15.back_ref = bf16[16,2,8,1664]{3,2,1,0:T(8,128)(2,1)S(1)} all-to-all(bf16[16,2,8,1664]{3,2,1,0:T(8,128)(2,1)S(1)} %relay.1), channel_id=1, replica_groups=mesh['rep'=16,'fsdp'=16] {'rep'}, dimensions={0} | all-to-all | bytes 1703936 | tf_op jit(solution)/shard_map/all_to_all | solution.py:277
  80.0 1.2 weights.1
  81.2 3.9 %collective-permute-start.6 = (bf16[2,8,6400]{2,1,0:T(8,128)(2,1)S(1)}, bf16[2,8,6400]{2,1,0:T(8,128)(2,1)S(1)}, u32[]{:S(2)}, u32[]{:S(2)}) collective-permute-start(bf16[2,8,6400]{2,1,0:T(8,128)(2,1)S(1)} %get-tuple-element.20), channel_id=1, source_target_pairs={{0,9},{1,8},{2,11},{3,10},{4,13},{5,12},{6,15},{7,14},{8,1},{9,0},... | collective-permute-start | bytes 614408 | tf_op jit(solution)/shard_map/ppermute | solution.py:274
  85.8 6.6 %collective-permute-done.6.refs_3_ = bf16[2,8,6400]{2,1,0:T(8,128)(2,1)S(1)} collective-permute-done((bf16[2,8,6400]{2,1,0:T(8,128)(2,1)S(1)}, bf16[2,8,6400]{2,1,0:T(8,128)(2,1)S(1)}, u32[]{:S(2)}, u32[]{:S(2)}) %collective-permute-start.6) | collective-permute-done | bytes 204832 | tf_op jit(solution)/shard_map/ppermute | solution.py:274
  92.5 2.8 %collective-permute-start.8 = (bf16[2,4,8,6400]{3,2,1,0:T(8,128)(2,1)S(1)}, bf16[2,4,8,6400]{3,2,1,0:T(8,128)(2,1)S(1)}, u32[]{:S(2)}, u32[]{:S(2)}) collective-permute-start(bf16[2,4,8,6400]{3,2,1,0:T(8,128)(2,1)S(1)} %chip.2.refs_0_), channel_id=1, source_target_pairs={{0,6},{1,7},{2,0},{3,1},{4,2},{5,3},{6,4},{7,5},{8,14},{9,15},{10,... | collective-permute-start | bytes 2457608 | tf_op jit(solution)/shard_map/ppermute | solution.py:274
  96.8 1.2 collective-permute-start.1
  98.1 5.2 %collective-permute-done.2.refs_2_ = bf16[2,8,6400]{2,1,0:T(8,128)(2,1)S(1)} collective-permute-done((bf16[2,8,6400]{2,1,0:T(8,128)(2,1)S(1)}, bf16[2,8,6400]{2,1,0:T(8,128)(2,1)S(1)}, u32[]{:S(2)}, u32[]{:S(2)}) %collective-permute-start.2) | collective-permute-done | bytes 204832 | tf_op jit(solution)/shard_map/ppermute | solution.py:274
  103.2 3.5 %collective-permute-done.3.refs_3_ = bf16[2,8,6400]{2,1,0:T(8,128)(2,1)S(1)} collective-permute-done((bf16[2,8,6400]{2,1,0:T(8,128)(2,1)S(1)}, bf16[2,8,6400]{2,1,0:T(8,128)(2,1)S(1)}, u32[]{:S(2)}, u32[]{:S(2)}) %collective-permute-start.3) | collective-permute-done | bytes 204832 | tf_op jit(solution)/shard_map/ppermute | solution.py:274
  106.7 5.9 %collective-permute-done.8.refs_5_.refs_2_ = bf16[2,4,8,6400]{3,2,1,0:T(8,128)(2,1)S(1)} collective-permute-done((bf16[2,4,8,6400]{3,2,1,0:T(8,128)(2,1)S(1)}, bf16[2,4,8,6400]{3,2,1,0:T(8,128)(2,1)S(1)}, u32[]{:S(2)}, u32[]{:S(2)}) %collective-permute-start.8) | collective-permute-done | bytes 819232 | tf_op jit(solution)/shard_map/ppermute | solution.py:274
  112.6 3.4 %collective-permute-done.7.refs_4_.refs_1_ = bf16[2,4,8,6400]{3,2,1,0:T(8,128)(2,1)S(1)} collective-permute-done((bf16[2,4,8,6400]{3,2,1,0:T(8,128)(2,1)S(1)}, bf16[2,4,8,6400]{3,2,1,0:T(8,128)(2,1)S(1)}, u32[]{:S(2)}, u32[]{:S(2)}) %collective-permute-start.7) | collective-permute-done | bytes 819232 | tf_op jit(solution)/shard_map/ppermute | solution.py:274
  117.7 18.2 %collective-permute-done.11.refs_2_ = bf16[2,4,8,6400]{3,2,1,0:T(8,128)(2,1)} collective-permute-done((bf16[2,4,8,6400]{3,2,1,0:T(8,128)(2,1)S(1)}, bf16[2,4,8,6400]{3,2,1,0:T(8,128)(2,1)}, u32[]{:S(2)}, u32[]{:S(2)}) %collective-permute-start.11) | collective-permute-done | bytes 819232 | tf_op jit(solution)/shard_map/ppermute | solution.py:274
  136.0 1.9 %collective-permute-start.12 = (bf16[2,4,8,6400]{3,2,1,0:T(8,128)(2,1)}, bf16[2,4,8,6400]{3,2,1,0:T(8,128)(2,1)}, u32[]{:S(2)}, u32[]{:S(2)}) collective-permute-start(bf16[2,4,8,6400]{3,2,1,0:T(8,128)(2,1)} %collective-permute-done.11.refs_2_), channel_id=1, source_target_pairs={{0,6},{1,7},{2,0},{3,1},{4,2},{5,3},{6,4},{7,5},{8,14},{9,15},{10,... | collective-permute-start | bytes 2457608 | tf_op jit(solution)/shard_map/ppermute | solution.py:274
  139.7 2.1 %momentum_relay.1 = bf16[16,8,1664]{2,1,0:T(8,128)(2,1)} custom-call(s32[2,16]{1,0:T(2,128)S(1)} %copy-done.15, bf16[16,3,8,1664]{3,2,1,0:T(8,128)(2,1)S(1)} %all-to-all-done.got_ref, bf16[2,4,8,6400]{3,2,1,0:T(8,128)(2,1)S(1)} %later.1.after_ref.refs_4_), custom_call_target="tpu_custom_call" | custom-call | flops 6144000 | bytes 1638400 | tf_op jit(solution)/shard_map/momentum_relay/pallas_call | solution.py:345
  141.7 6.1 %all-to-all-start.2 = ((bf16[16,8,1664]{2,1,0:T(8,128)(2,1)}), bf16[16,8,1664]{2,1,0:T(8,128)(2,1)S(1)}, u32[]{:S(2)}, u32[]{:S(2)}) async-start(bf16[16,8,1664]{2,1,0:T(8,128)(2,1)} %momentum_relay.1), calls=%async_computation.2 | async-start | bytes 851968 | tf_op jit(solution)/shard_map/all_to_all | solution.py:277
  147.8 1.1 copy-done.6
  149.0 1.1 copy-done.8
  150.1 1.1 copy-done.10
  151.3 1.1 copy-done.12
  152.4 2.9 %evaluate.2 = (bf16[2,1,64,25600]{3,2,1,0:T(8,128)(2,1)}, bf16[2,64,6400]{2,1,0:T(8,128)(2,1)}) custom-call(s32[1]{0:T(128)} %bitcast.core_ref, bf16[2,128,128]{2,1,0:T(8,128)(2,1)S(1)} %broadcast_select_fusion.tokens_ref, bf16[2,4,8,6400]{3,2,1,0:T(8,128)(2,1)S(1)} %copy-done.6, bf16[2,4,8,6400]{3,2,1,0:T(8,128)(2,1)S(1)} %copy-done.10, ...), custom_call_target="tpu_custom_call" | custom-call | flops 419430400 | bytes 3276800 | tf_op jit(solution)/shard_map/evaluate/pallas_call | solution.py:368
  155.4 2.1 %collective-permute-start.14 = (bf16[2,64,6400]{2,1,0:T(8,128)(2,1)}, bf16[2,64,6400]{2,1,0:T(8,128)(2,1)}, u32[]{:S(2)}, u32[]{:S(2)}) collective-permute-start(bf16[2,64,6400]{2,1,0:T(8,128)(2,1)} %get-tuple-element.23), channel_id=1, source_target_pairs={{0,1},{1,0},{2,3},{3,2},{4,5},{5,4},{6,7},{7,6},{8,9},{9,8},{10,11... | collective-permute-start | bytes 4915208 | tf_op jit(solution)/shard_map/ppermute | solution.py:274
  157.4 5.0 %all-to-all-done.2.back_ref = bf16[16,8,1664]{2,1,0:T(8,128)(2,1)S(1)} async-done(((bf16[16,8,1664]{2,1,0:T(8,128)(2,1)}), bf16[16,8,1664]{2,1,0:T(8,128)(2,1)S(1)}, u32[]{:S(2)}, u32[]{:S(2)}) %all-to-all-start.2) | async-done | bytes 426016 | tf_op jit(solution)/shard_map/all_to_all | solution.py:277
  164.6 3.4 %evaluate.3 = (bf16[2,1,64,25600]{3,2,1,0:T(8,128)(2,1)}, bf16[2,64,6400]{2,1,0:T(8,128)(2,1)S(1)}) custom-call(s32[1]{0:T(128)} %bitcast.core_ref, bf16[2,128,128]{2,1,0:T(8,128)(2,1)S(1)} %broadcast_select_fusion.tokens_ref, bf16[2,4,8,6400]{3,2,1,0:T(8,128)(2,1)S(1)} %copy-done.1, ...), custom_call_target="tpu_custom_call", output_to_operand_aliasing={{0}: (7, {})} | custom-call | flops 419430400 | bytes 3276800 | tf_op jit(solution)/shard_map/evaluate/pallas_call | solution.py:368
  168.0 2.3 %collective-permute-start.13 = (bf16[2,64,6400]{2,1,0:T(8,128)(2,1)S(1)}, bf16[2,64,6400]{2,1,0:T(8,128)(2,1)S(1)}, u32[]{:S(2)}, u32[]{:S(2)}) collective-permute-start(bf16[2,64,6400]{2,1,0:T(8,128)(2,1)S(1)} %get-tuple-element.22), channel_id=1, source_target_pairs={{0,1},{1,0},{2,3},{3,2},{4,5},{5,4},{6,7},{7,6},{8,9},{9,8},{10,11... | collective-permute-start | bytes 4915208 | tf_op jit(solution)/shard_map/ppermute | solution.py:274
  170.3 2.7 %place.2.buffer_ref = bf16[2,1,64,25600]{3,2,1,0:T(8,128)(2,1)} custom-call(s32[1]{0:T(128)} %bitcast.core_ref, bf16[2,64,6400]{2,1,0:T(8,128)(2,1)} %collective-permute-done.14.piece_ref, bf16[2,1,64,25600]{3,2,1,0:T(8,128)(2,1)} %get-tuple-element.24.buffer_ref), custom_call_target="tpu_custom_call", output_to_operand_aliasing={{}: (2, {})} | custom-call | bytes 1638400 | tf_op jit(solution)/shard_map/place/pallas_call | solution.py:384
  173.4 1.2 place.3
  (63 shorter events, 10.9 us)
Async XLA Ops:
  5.4 11.8 %copy-start.16 = (bf16[2,1,64,128]{3,2,1,0:T(8,128)(2,1)S(1)}, bf16[2,1,64,128]{3,2,1,0:T(8,128)(2,1)}, u32[]{:S(2)}) copy-start(bf16[2,1,64,128]{3,2,1,0:T(8,128)(2,1)} %param.12) | copy-start | bytes 98308
  5.4 13.3 %copy-start.2 = (f32[1,8,25600]{2,1,0:T(8,128)S(1)}, f32[1,8,25600]{2,1,0:T(8,128)}, u32[]{:S(2)}) copy-start(f32[1,8,25600]{2,1,0:T(8,128)} %m_ref.1) | copy-start | bytes 2457604
  5.4 41.9 %all-to-all-start = ((bf16[16,3,8,1664]{3,2,1,0:T(8,128)(2,1)}), bf16[16,3,8,1664]{3,2,1,0:T(8,128)(2,1)S(1)}, u32[]{:S(2)}, u32[]{:S(2)}) async-start(bf16[16,3,8,1664]{3,2,1,0:T(8,128)(2,1)} %get-tuple-element.14), calls=%async_computation | async-start | bytes 2555904 | tf_op jit(solution)/shard_map/all_to_all | solution.py:277
  17.3 6.1 %collective-permute-start = (bf16[2,64,128]{1,2,0:T(8,128)(2,1)S(1)}, bf16[2,64,128]{1,2,0:T(8,128)(2,1)S(1)}, u32[]{:S(2)}, u32[]{:S(2)}) collective-permute-start(bf16[2,64,128]{1,2,0:T(8,128)(2,1)S(1)} %bitcast.43), channel_id=1, source_target_pairs={{0,1},{1,0},{2,3},{3,2},{4,5},{5,4},{6,7},{7,6},{8,9},{9,8},{10,11... | collective-permute-start | bytes 98312 | tf_op jit(solution)/shard_map/ppermute | solution.py:274
  18.8 1.1 copy-start.3
  19.9 1.1 copy-start.4
  23.4 24.0 %copy-start.15 = (s32[2,16]{1,0:T(2,128)S(1)}, s32[2,16]{1,0:T(2,128)}, u32[]{:S(2)}) copy-start(s32[2,16]{1,0:T(2,128)} %matching_ref.3) | copy-start | bytes 388
  24.2 55.8 %copy-start.14 = (f32[8,25600]{1,0:T(8,128)S(1)}, f32[8,25600]{1,0:T(8,128)}, u32[]{:S(2)}) copy-start(f32[8,25600]{1,0:T(8,128)} %get-tuple-element.15.d1_ref) | copy-start | bytes 2457604
  81.2 4.6 %collective-permute-start.5 = (bf16[2,8,6400]{2,1,0:T(8,128)(2,1)S(1)}, bf16[2,8,6400]{2,1,0:T(8,128)(2,1)S(1)}, u32[]{:S(2)}, u32[]{:S(2)}) collective-permute-start(bf16[2,8,6400]{2,1,0:T(8,128)(2,1)S(1)} %get-tuple-element.19.refs_0_), channel_id=1, source_target_pairs={{0,8},{1,9},{2,10},{3,11},{4,12},{5,13},{6,14},{7,15},{8,0},{9,1},... | collective-permute-start | bytes 614408 | tf_op jit(solution)/shard_map/ppermute | solution.py:274
  81.2 11.2 %collective-permute-start.6 = (bf16[2,8,6400]{2,1,0:T(8,128)(2,1)S(1)}, bf16[2,8,6400]{2,1,0:T(8,128)(2,1)S(1)}, u32[]{:S(2)}, u32[]{:S(2)}) collective-permute-start(bf16[2,8,6400]{2,1,0:T(8,128)(2,1)S(1)} %get-tuple-element.20), channel_id=1, source_target_pairs={{0,9},{1,8},{2,11},{3,10},{4,13},{5,12},{6,15},{7,14},{8,1},{9,0},... | collective-permute-start | bytes 614408 | tf_op jit(solution)/shard_map/ppermute | solution.py:274
  85.1 7.3 %collective-permute-start.4 = (bf16[2,8,6400]{2,1,0:T(8,128)(2,1)S(1)}, bf16[2,8,6400]{2,1,0:T(8,128)(2,1)S(1)}, u32[]{:S(2)}, u32[]{:S(2)}) collective-permute-start(bf16[2,8,6400]{2,1,0:T(8,128)(2,1)S(1)} %get-tuple-element.20), channel_id=1, source_target_pairs={{0,1},{1,0},{2,3},{3,2},{4,5},{5,4},{6,7},{7,6},{8,9},{9,8},{10,11... | collective-permute-start | bytes 614408 | tf_op jit(solution)/shard_map/ppermute | solution.py:274
  92.5 20.1 %collective-permute-start.8 = (bf16[2,4,8,6400]{3,2,1,0:T(8,128)(2,1)S(1)}, bf16[2,4,8,6400]{3,2,1,0:T(8,128)(2,1)S(1)}, u32[]{:S(2)}, u32[]{:S(2)}) collective-permute-start(bf16[2,4,8,6400]{3,2,1,0:T(8,128)(2,1)S(1)} %chip.2.refs_0_), channel_id=1, source_target_pairs={{0,6},{1,7},{2,0},{3,1},{4,2},{5,3},{6,4},{7,5},{8,14},{9,15},{10,... | collective-permute-start | bytes 2457608 | tf_op jit(solution)/shard_map/ppermute | solution.py:274
  95.3 20.7 %collective-permute-start.7 = (bf16[2,4,8,6400]{3,2,1,0:T(8,128)(2,1)S(1)}, bf16[2,4,8,6400]{3,2,1,0:T(8,128)(2,1)S(1)}, u32[]{:S(2)}, u32[]{:S(2)}) collective-permute-start(bf16[2,4,8,6400]{3,2,1,0:T(8,128)(2,1)S(1)} %chip.2.refs_0_), channel_id=1, source_target_pairs={{0,2},{1,3},{2,4},{3,5},{4,6},{5,7},{6,0},{7,1},{8,10},{9,11},{10,... | collective-permute-start | bytes 2457608 | tf_op jit(solution)/shard_map/ppermute | solution.py:274
  96.2 7.0 %collective-permute-start.2 = (bf16[2,8,6400]{2,1,0:T(8,128)(2,1)S(1)}, bf16[2,8,6400]{2,1,0:T(8,128)(2,1)S(1)}, u32[]{:S(2)}, u32[]{:S(2)}) collective-permute-start(bf16[2,8,6400]{2,1,0:T(8,128)(2,1)S(1)} %get-tuple-element.17.refs_0_), channel_id=1, source_target_pairs={{0,8},{1,9},{2,10},{3,11},{4,12},{5,13},{6,14},{7,15},{8,0},{9,1},... | collective-permute-start | bytes 614408 | tf_op jit(solution)/shard_map/ppermute | solution.py:274
  96.4 10.3 %collective-permute-start.3 = (bf16[2,8,6400]{2,1,0:T(8,128)(2,1)S(1)}, bf16[2,8,6400]{2,1,0:T(8,128)(2,1)S(1)}, u32[]{:S(2)}, u32[]{:S(2)}) collective-permute-start(bf16[2,8,6400]{2,1,0:T(8,128)(2,1)S(1)} %get-tuple-element.18), channel_id=1, source_target_pairs={{0,9},{1,8},{2,11},{3,10},{4,13},{5,12},{6,15},{7,14},{8,1},{9,0},... | collective-permute-start | bytes 614408 | tf_op jit(solution)/shard_map/ppermute | solution.py:274
  96.8 9.9 %collective-permute-start.1 = (bf16[2,8,6400]{2,1,0:T(8,128)(2,1)S(1)}, bf16[2,8,6400]{2,1,0:T(8,128)(2,1)S(1)}, u32[]{:S(2)}, u32[]{:S(2)}) collective-permute-start(bf16[2,8,6400]{2,1,0:T(8,128)(2,1)S(1)} %get-tuple-element.18), channel_id=1, source_target_pairs={{0,1},{1,0},{2,3},{3,2},{4,5},{5,4},{6,7},{7,6},{8,9},{9,8},{10,11... | collective-permute-start | bytes 614408 | tf_op jit(solution)/shard_map/ppermute | solution.py:274
  112.6 3.5 %copy-start.7 = (bf16[2,4,8,6400]{3,2,1,0:T(8,128)(2,1)}, bf16[2,4,8,6400]{3,2,1,0:T(8,128)(2,1)S(1)}, u32[]{:S(2)}) copy-start(bf16[2,4,8,6400]{3,2,1,0:T(8,128)(2,1)S(1)} %collective-permute-done.8.refs_5_.refs_2_) | copy-start | bytes 2457604
  116.0 20.0 %collective-permute-start.11 = (bf16[2,4,8,6400]{3,2,1,0:T(8,128)(2,1)S(1)}, bf16[2,4,8,6400]{3,2,1,0:T(8,128)(2,1)}, u32[]{:S(2)}, u32[]{:S(2)}) collective-permute-start(bf16[2,4,8,6400]{3,2,1,0:T(8,128)(2,1)S(1)} %chip.3.from_ref.refs_0_), channel_id=1, source_target_pairs={{0,6},{1,7},{2,0},{3,1},{4,2},{5,3},{6,4},{7,5},{8,14},{9,15},{10,... | collective-permute-start | bytes 2457608 | tf_op jit(solution)/shard_map/ppermute | solution.py:274
  116.8 21.0 %collective-permute-start.9 = (bf16[2,4,8,6400]{3,2,1,0:T(8,128)(2,1)S(1)}, bf16[2,4,8,6400]{3,2,1,0:T(8,128)(2,1)S(1)}, u32[]{:S(2)}, u32[]{:S(2)}) collective-permute-start(bf16[2,4,8,6400]{3,2,1,0:T(8,128)(2,1)S(1)} %collective-permute-done.7.refs_4_.refs_1_), channel_id=1, source_target_pairs={{0,2},{1,3},{2,4},{3,5},{4,6},{5,7},{6,0},{7,1},{8,10},{9,11},{10,... | collective-permute-start | bytes 2457608 | tf_op jit(solution)/shard_map/ppermute | solution.py:274
  136.0 27.5 %collective-permute-start.12 = (bf16[2,4,8,6400]{3,2,1,0:T(8,128)(2,1)}, bf16[2,4,8,6400]{3,2,1,0:T(8,128)(2,1)}, u32[]{:S(2)}, u32[]{:S(2)}) collective-permute-start(bf16[2,4,8,6400]{3,2,1,0:T(8,128)(2,1)} %collective-permute-done.11.refs_2_), channel_id=1, source_target_pairs={{0,6},{1,7},{2,0},{3,1},{4,2},{5,3},{6,4},{7,5},{8,14},{9,15},{10,... | collective-permute-start | bytes 2457608 | tf_op jit(solution)/shard_map/ppermute | solution.py:274
  137.9 0.9 copy-start.11
  138.8 0.9 copy-start
  139.7 23.8 %collective-permute-start.10 = (bf16[2,4,8,6400]{3,2,1,0:T(8,128)(2,1)S(1)}, bf16[2,4,8,6400]{3,2,1,0:T(8,128)(2,1)}, u32[]{:S(2)}, u32[]{:S(2)}) collective-permute-start(bf16[2,4,8,6400]{3,2,1,0:T(8,128)(2,1)S(1)} %later.1.after_ref.refs_4_), channel_id=1, source_target_pairs={{0,2},{1,3},{2,4},{3,5},{4,6},{5,7},{6,0},{7,1},{8,10},{9,11},{10,... | collective-permute-start | bytes 2457608 | tf_op jit(solution)/shard_map/ppermute | solution.py:274
  141.7 20.8 %all-to-all-start.2 = ((bf16[16,8,1664]{2,1,0:T(8,128)(2,1)}), bf16[16,8,1664]{2,1,0:T(8,128)(2,1)S(1)}, u32[]{:S(2)}, u32[]{:S(2)}) async-start(bf16[16,8,1664]{2,1,0:T(8,128)(2,1)} %momentum_relay.1), calls=%async_computation.2 | async-start | bytes 851968 | tf_op jit(solution)/shard_map/all_to_all | solution.py:277
  147.8 1.1 copy-start.6
  149.0 1.1 copy-start.8
  150.1 1.1 copy-start.10
  151.2 1.1 copy-start.12
  155.3 8.1 %copy-start.1 = (bf16[2,4,8,6400]{3,2,1,0:T(8,128)(2,1)S(1)}, bf16[2,4,8,6400]{3,2,1,0:T(8,128)(2,1)}, u32[]{:S(2)}) copy-start(bf16[2,4,8,6400]{3,2,1,0:T(8,128)(2,1)} %copy-done) | copy-start | bytes 2457604
  155.4 15.0 %collective-permute-start.14 = (bf16[2,64,6400]{2,1,0:T(8,128)(2,1)}, bf16[2,64,6400]{2,1,0:T(8,128)(2,1)}, u32[]{:S(2)}, u32[]{:S(2)}) collective-permute-start(bf16[2,64,6400]{2,1,0:T(8,128)(2,1)} %get-tuple-element.23), channel_id=1, source_target_pairs={{0,1},{1,0},{2,3},{3,2},{4,5},{5,4},{6,7},{7,6},{8,9},{9,8},{10,11... | collective-permute-start | bytes 4915208 | tf_op jit(solution)/shard_map/ppermute | solution.py:274
  163.5 1.1 copy-start.13
  168.0 5.5 %collective-permute-start.13 = (bf16[2,64,6400]{2,1,0:T(8,128)(2,1)S(1)}, bf16[2,64,6400]{2,1,0:T(8,128)(2,1)S(1)}, u32[]{:S(2)}, u32[]{:S(2)}) collective-permute-start(bf16[2,64,6400]{2,1,0:T(8,128)(2,1)S(1)} %get-tuple-element.22), channel_id=1, source_target_pairs={{0,1},{1,0},{2,3},{3,2},{4,5},{5,4},{6,7},{7,6},{8,9},{9,8},{10,11... | collective-permute-start | bytes 4915208 | tf_op jit(solution)/shard_map/ppermute | solution.py:274
  (2 other events, 1.8 us)

commit v2 on v1

--- a/solution.py
+++ b/solution.py
@@ -118,7 +118,8 @@
         back_ref[r, 1] = (0.5 * (held_ref[r] + held_ref[matching_ref[1, r]])).astype(BF16)
 
 
-def momentum_relay_kernel(matching_ref, got_ref, after_ref, back_ref, held_ref):
+def momentum_relay_kernel(matching_ref, got_ref, *refs):
+    back_ref, held_ref = refs[-2:]
     replicas = got_ref.shape[0]
 
     @pl.loop(0, replicas)
@@ -136,7 +137,7 @@
 
 
 def weights_kernel(core_ref, back_ref, d1_ref, d2_ref, *refs):
-    parts, w_ref = refs[:4], refs[4]
+    parts, (own_ref, w_ref) = refs[:4], refs[4:]
     slab = d1_ref.shape[1] // SLABS
     for j in range(SLABS):
         lanes = pl.ds(j * slab, slab)
@@ -154,6 +155,11 @@
                 part[0, :, lanes] = first.astype(BF16)
                 part[1, :, lanes] = second.astype(BF16)
 
+        @pl.when(mine)
+        def _(quarter=quarter, lanes=lanes, first=first, second=second):
+            own_ref[quarter, 0, :, lanes] = first.astype(BF16)
+            own_ref[quarter, 1, :, lanes] = second.astype(BF16)
+
 
 def momentum_kernel(back_ref, d_ref, u_ref):
     slab = d_ref.shape[1] // SLABS
@@ -162,13 +168,22 @@
         u_ref[0, :, lanes] = joined(back_ref[2 * j], back_ref[2 * j + 1], slab) + d_ref[:, lanes]
 
 
-def copy_kernel(from_ref, after_ref, to_ref):
-    for step in range(to_ref.shape[0]):
-        to_ref[step] = from_ref[step]
+def onward_kernel(quarter, own_ref, others_ref, *refs):
+    out_ref = refs[-1]
+    for step in range(out_ref.shape[0]):
+        out_ref[step, 0] = own_ref[quarter, step]
+        for i in range(3):
+            out_ref[step, i + 1] = others_ref[step, i]
+
+
+def low_chip_kernel(*refs):
+    chip_kernel(*refs[:3], refs[-3])
+    for part, later in zip(refs[3:5], refs[-2:]):
+        later[...] = part[...]
 
 
 def chip_kernel(*refs):
-    pieces, out = refs[:4], refs[-1]
+    pieces, out = refs[:3], refs[-1]
     for i, piece in enumerate(pieces):
         for step in range(out.shape[0]):
             out[step, i] = piece[step]
@@ -178,7 +193,7 @@
 
 
 def evaluate_kernel(quarter, core_ref, tokens_ref, *refs):
-    blocks, (out_ref, sent_ref, own_ref, done) = refs[:4], refs[-4:]
+    blocks, far_ref, (out_ref, sent_ref, own_ref, done) = refs[:6], refs[6], refs[-4:]
     steps, tokens, width = sent_ref.shape
     tile = width // TILES
     start = pl.multiple_of(core_ref[0] * (2 * width) + quarter * width, LANES)
@@ -186,7 +201,12 @@
     for step in range(steps):
         for j in range(TILES):
             lanes = pl.ds(j * tile, tile)
-            rows = jnp.concatenate([block[step, i, :, lanes] for block in blocks for i in range(4)], axis=0)
+            rows = []
+            for own, others in zip(blocks[::2], blocks[1::2]):
+                rows.append(own[quarter, step, :, lanes])
+                rows += [others[step, i, :, lanes] for i in range(3)]
+            rows += [far_ref[step, i, :, lanes] for i in range(4)]
+            rows = jnp.concatenate(rows, axis=0)
             product = jnp.dot(tokens_ref[step], rows, preferred_element_type=F32).astype(BF16)
             own_ref[step, :, lanes] = product[:tokens]
             sent_ref[step, :, lanes] = product[tokens:]
@@ -242,7 +262,8 @@
     flat = jax.ShapeDtypeStruct((rows, columns), F32)
     whole_out = jax.ShapeDtypeStruct((1, rows, columns), F32)
     part = jax.ShapeDtypeStruct((steps, rows, quarter), BF16)
-    chip = jax.ShapeDtypeStruct((steps, 4, rows, quarter), BF16)
+    chip = jax.ShapeDtypeStruct((steps, 3, rows, quarter), BF16)
+    own_rows = jax.ShapeDtypeStruct((2, steps, rows, quarter), BF16)
     moved = jax.ShapeDtypeStruct((replicas, 3, rows, window), BF16)
     two_backs = jax.ShapeDtypeStruct((replicas, 2, rows, window), BF16)
     one_back = jax.ShapeDtypeStruct((replicas, rows, window), BF16)
@@ -318,40 +339,55 @@
         10 * unit,
         scratch_shapes=[pltpu.VMEM((replicas, rows, window), F32)],
     )(matching, got, d2, chip_tokens)
-    kept_low, sent_low, kept_high, sent_high, anchor_out = call(
+    kept_low, sent_low, kept_high, sent_high, own, anchor_out = call(
         weights_kernel,
         "weights",
         [scalar, whole, whole, whole],
-        [whole] * 5,
-        [part] * 4 + [whole_out],
+        [whole] * 6,
+        [part] * 4 + [own_rows, whole_out],
         8 * unit,
         24 * unit,
     )(core_ref, relayed(back), d1, d2)
 
-    def chip_rows(kept, sent, *after):
-        pieces = kept, permute(sent, dc=1), permute(kept, dz=1), permute(sent, dz=1, dc=1)
-        return call(
-            chip_kernel, "chip", [whole] * 4 + [loose] * len(after), whole, chip, 0, 8 * unit
-        )(*pieces, *after)
-
-    low = chip_rows(kept_low, sent_low)
+    def to_chip(kept, sent):
+        return permute(sent, dc=1), permute(kept, dz=1), permute(sent, dz=1, dc=1)
+
+    own_up, own_down = permute(own, dy=1), permute(own, dy=-1)
+    low, kept_high, sent_high = call(
+        low_chip_kernel,
+        "low_chip",
+        [whole] * 5 + [loose] * 2,
+        [whole] * 3,
+        [chip, part, part],
+        0,
+        10 * unit,
+    )(*to_chip(kept_low, sent_low), kept_high, sent_high, own_up, own_down)
     low_up, low_down = permute(low, dy=1), permute(low, dy=-1)
-    low_far = permute(low_up, dy=1)
-    high = chip_rows(kept_high, sent_high, low_up, low_down)
-    high_down = permute(high, dy=-1)
-    later_high = call(copy_kernel, "later", [whole, loose], whole, chip, 0, 8 * unit)(high, low_far)
-    high_up = permute(later_high, dy=1)
-    high_far = permute(high_down, dy=-1)
+    high = call(chip_kernel, "chip", [whole] * 3 + [loose], whole, chip, 0, 6 * unit)(
+        *to_chip(kept_high, sent_high), low_down
+    )
+    high_down, high_up = permute(high, dy=-1), permute(high, dy=1)
+    far_rows = jax.ShapeDtypeStruct((steps, 4, rows, quarter), BF16)
+
+    def onward(at_quarter, own, others, *after):
+        kernel = functools.partial(onward_kernel, at_quarter)
+        in_specs = [whole] * 2 + [loose] * len(after)
+        return call(kernel, "onward", in_specs, whole, far_rows, 0, 8 * unit)(own, others, *after)
+
+    low_onward = onward(0, own_up, low_up)
+    low_far = permute(low_onward, dy=1)
+    high_onward = onward(1, own_down, high_down, high_up)
+    high_far = permute(high_onward, dy=-1)
     last = call(
         momentum_relay_kernel,
         "momentum_relay",
-        [scalar, whole, loose],
+        [scalar, whole, loose, loose],
         whole,
         one_back,
         30 * unit,
         8 * unit,
         scratch_shapes=[pltpu.VMEM((replicas, rows, window), F32)],
-    )(matching, got, later_high)
+    )(matching, got, low_onward, high)
     momentum_out = call(momentum_kernel, "momentum", [whole] * 2, whole, whole_out, 2 * unit, 10 * unit)(
         relayed(last), d2
     )
@@ -359,7 +395,7 @@
     def evaluate(at_quarter, blocks, buffer, *after):
         kernel = functools.partial(evaluate_kernel, at_quarter)
         operands = [core_ref, chip_tokens, *blocks, *after]
-        in_specs = [scalar] + [whole] * 5 + [loose] * len(after)
+        in_specs = [scalar] + [whole] * 8 + [loose] * len(after)
         aliases = {}
         if buffer is not None:
             aliases = {len(operands): 0}
@@ -393,8 +429,10 @@
             scratch_shapes=[pltpu.SemaphoreType.DMA((steps, TILES))],
         )(core_ref, piece, buffer)
 
-    buffer, low_sent = evaluate(0, (low, low_up, low_down, low_far), None, later_high)
-    buffer, high_sent = evaluate(1, (high, high_up, high_down, high_far), buffer, momentum_out)
+    lows = own, low, own_up, low_up, own_down, low_down, low_far
+    highs = own, high, own_up, high_up, own_down, high_down, high_far
+    buffer, low_sent = evaluate(0, lows, None, high_onward)
+    buffer, high_sent = evaluate(1, highs, buffer, momentum_out)
     buffer = put(0, permute(low_sent, dc=1), buffer)
     buffer = put(1, permute(high_sent, dc=1), buffer)
     return anchor_out, momentum_out, buffer

time: 176 us -> 164 us (0.932)
  waiting for transfers between devices: 72 us -> 66.3 us
  local copies, waits for them, and re-layouts: 12.1 us -> 7.74 us
    ppermute x15 -> x17, waiting for transfers between devices: 43.9 us -> 34.8 us  [permute(): return lax.ppermute(value, 'fsdp', pairs)]
    unnamed x35 -> x37, local copies, waits for them, and re-layouts: 11 us -> 6.66 us
    all_to_all x2, waiting for transfers between devices: 28.1 us -> 31.5 us  [relayed(): return lax.all_to_all(value, 'rep', 0, 0, tiled=True)]
    ppermute x15 -> x17, starting transfers between devices: 17.4 us -> 17.3 us  [permute(): return lax.ppermute(value, 'fsdp', pairs)]
  transfers between devices with their start and end apart: 17 -> 19, of which waited for: 10 -> 12; matrix products, arithmetic and copies ran while one was open for 1% -> 1% of each run, Pallas kernels for 8% -> 9%
where the time goes in v2:
time: 164 us
  waiting for transfers between devices  66.3 us (40%)
  starting transfers between devices  34.4 us (21%)
  blocking collectives  31.4 us (19%)
  Pallas kernels  22.7 us (14%)
  local copies, waits for them, and re-layouts  7.74 us (5%)
    ppermute x17, waiting for transfers between devices, permute(): return lax.ppermute(value, 'fsdp', pairs)  34.8 us
    all_to_all x2, waiting for transfers between devices, relayed(): return lax.all_to_all(value, 'rep', 0, 0, tiled=True)  31.5 us
    all_to_all x1, blocking collectives, relayed(): return lax.all_to_all(value, 'rep', 0, 0, tiled=True)  31.4 us
    ppermute x17, starting transfers between devices, permute(): return lax.ppermute(value, 'fsdp', pairs)  17.3 us
    all_to_all x2, starting transfers between devices, relayed(): return lax.all_to_all(value, 'rep', 0, 0, tiled=True)  17.1 us
    unnamed x37, local copies, waits for them, and re-layouts  6.66 us
    pallas_call x2, Pallas kernels, evaluate(): call(kernel, 'evaluate', in_specs, [far, whole], [products, sent_products...  6.15 us
    pallas_call x1, Pallas kernels, shards(): call(pack_kernel, 'pack', [far] * 5, [whole] * 2, [moved, flat], 100 * un...  4.76 us
  transfers between devices with their start and end apart: 19, of which 12 were waited for; matrix products, arithmetic and copies ran while one was open for 1% of the time, Pallas kernels for 9%

profile of v2, /device:TPU:1, one launch (start us, length us, event | category | flops | bytes accessed | tf_op | source)
XLA Modules:
  0.0 163.7 jit_solution(9191742817453209272)
XLA Ops:
  0.6 4.8 %pack.1 = (bf16[16,3,8,1664]{3,2,1,0:T(8,128)(2,1)}, f32[8,25600]{1,0:T(8,128)}) custom-call(f32[1,8,25600]{2,1,0:T(8,128)} %refs_0_.1, f32[1,8,25600]{2,1,0:T(8,128)} %refs_1_.1, f32[1,8,25600]{2,1,0:T(8,128)} %m_ref.1, f32[1,8,25600]{2,1,0:T(8,128)} %v_ref.1, bf16[2,1,8,25600]{3,2,1,0:T(8,128)(2,1)} %g_ref.1), custom_call_target="tpu_custom_call" | custom-call | flops 20480000 | bytes 5324800 | tf_op jit(solution)/shard_map/pack/pallas_call | solution.py:315
  5.4 11.7 %all-to-all-start = ((bf16[16,3,8,1664]{3,2,1,0:T(8,128)(2,1)}), bf16[16,3,8,1664]{3,2,1,0:T(8,128)(2,1)S(1)}, u32[]{:S(2)}, u32[]{:S(2)}) async-start(bf16[16,3,8,1664]{3,2,1,0:T(8,128)(2,1)} %get-tuple-element.18), calls=%async_computation | async-start | bytes 2555904 | tf_op jit(solution)/shard_map/all_to_all | solution.py:298
  18.8 1.1 copy-done.2
  19.9 1.1 copy-done.3
  21.1 2.3 %second.1.d_ref.d2_ref = f32[8,25600]{1,0:T(8,128)S(1)} custom-call(f32[1,8,25600]{2,1,0:T(8,128)S(1)} %copy-done.1, f32[1,8,25600]{2,1,0:T(8,128)S(1)} %copy-done.2, bf16[2,1,8,25600]{3,2,1,0:T(8,128)(2,1)S(1)} %copy-done.3), custom_call_target="tpu_custom_call" | custom-call | flops 24576000 | bytes 2867200 | tf_op jit(solution)/shard_map/second/pallas_call | solution.py:328
  24.2 23.1 %all-to-all-done.got_ref = bf16[16,3,8,1664]{3,2,1,0:T(8,128)(2,1)S(1)} async-done(((bf16[16,3,8,1664]{3,2,1,0:T(8,128)(2,1)}), bf16[16,3,8,1664]{3,2,1,0:T(8,128)(2,1)S(1)}, u32[]{:S(2)}, u32[]{:S(2)}) %all-to-all-start) | async-done | bytes 1277984 | tf_op jit(solution)/shard_map/all_to_all | solution.py:298
  47.4 1.3 relay.1
  48.7 31.4 %all_to_all.15.back_ref = bf16[16,2,8,1664]{3,2,1,0:T(8,128)(2,1)S(1)} all-to-all(bf16[16,2,8,1664]{3,2,1,0:T(8,128)(2,1)S(1)} %relay.1), channel_id=1, replica_groups=mesh['rep'=16,'fsdp'=16] {'rep'}, dimensions={0} | all-to-all | bytes 1703936 | tf_op jit(solution)/shard_map/all_to_all | solution.py:298
  80.0 1.2 weights.1
  81.3 2.7 %collective-permute-start.5 = (bf16[2,2,8,6400]{3,2,1,0:T(8,128)(2,1)S(1)}, bf16[2,2,8,6400]{3,2,1,0:T(8,128)(2,1)S(1)}, u32[]{:S(2)}, u32[]{:S(2)}) collective-permute-start(bf16[2,2,8,6400]{3,2,1,0:T(8,128)(2,1)S(1)} %get-tuple-element.21.refs_0_), channel_id=1, source_target_pairs={{0,6},{1,7},{2,0},{3,1},{4,2},{5,3},{6,4},{7,5},{8,14},{9,15},{10,... | collective-permute-start | bytes 1228808 | tf_op jit(solution)/shard_map/ppermute | solution.py:295
  84.8 4.2 %collective-permute-start.4 = (bf16[2,8,6400]{2,1,0:T(8,128)(2,1)S(1)}, bf16[2,8,6400]{2,1,0:T(8,128)(2,1)S(1)}, u32[]{:S(2)}, u32[]{:S(2)}) collective-permute-start(bf16[2,8,6400]{2,1,0:T(8,128)(2,1)S(1)} %get-tuple-element.22), channel_id=1, source_target_pairs={{0,9},{1,8},{2,11},{3,10},{4,13},{5,12},{6,15},{7,14},{8,1},{9,0},... | collective-permute-start | bytes 614408 | tf_op jit(solution)/shard_map/ppermute | solution.py:295
  89.7 6.8 %collective-permute-done.4.refs_2_ = bf16[2,8,6400]{2,1,0:T(8,128)(2,1)S(1)} collective-permute-done((bf16[2,8,6400]{2,1,0:T(8,128)(2,1)S(1)}, bf16[2,8,6400]{2,1,0:T(8,128)(2,1)S(1)}, u32[]{:S(2)}, u32[]{:S(2)}) %collective-permute-start.4) | collective-permute-done | bytes 204832 | tf_op jit(solution)/shard_map/ppermute | solution.py:295
  96.6 2.7 %collective-permute-start.10 = (bf16[2,3,8,6400]{3,2,1,0:T(8,128)(2,1)S(1)}, bf16[2,3,8,6400]{3,2,1,0:T(8,128)(2,1)S(1)}, u32[]{:S(2)}, u32[]{:S(2)}) collective-permute-start(bf16[2,3,8,6400]{3,2,1,0:T(8,128)(2,1)S(1)} %get-tuple-element.26.refs_1_), channel_id=1, source_target_pairs={{0,6},{1,7},{2,0},{3,1},{4,2},{5,3},{6,4},{7,5},{8,14},{9,15},{10,... | collective-permute-start | bytes 1843208 | tf_op jit(solution)/shard_map/ppermute | solution.py:295
  100.0 1.2 collective-permute-start.7
  101.2 5.2 %collective-permute-done.8.refs_1_ = bf16[2,8,6400]{2,1,0:T(8,128)(2,1)S(1)} collective-permute-done((bf16[2,8,6400]{2,1,0:T(8,128)(2,1)S(1)}, bf16[2,8,6400]{2,1,0:T(8,128)(2,1)S(1)}, u32[]{:S(2)}, u32[]{:S(2)}) %collective-permute-start.8) | collective-permute-done | bytes 204832 | tf_op jit(solution)/shard_map/ppermute | solution.py:295
  106.4 3.5 %collective-permute-done.9.refs_2_ = bf16[2,8,6400]{2,1,0:T(8,128)(2,1)S(1)} collective-permute-done((bf16[2,8,6400]{2,1,0:T(8,128)(2,1)S(1)}, bf16[2,8,6400]{2,1,0:T(8,128)(2,1)S(1)}, u32[]{:S(2)}, u32[]{:S(2)}) %collective-permute-start.9) | collective-permute-done | bytes 204832 | tf_op jit(solution)/shard_map/ppermute | solution.py:295
  109.9 2.3 %collective-permute-done.10.refs_3_.refs_5_ = bf16[2,3,8,6400]{3,2,1,0:T(8,128)(2,1)S(1)} collective-permute-done((bf16[2,3,8,6400]{3,2,1,0:T(8,128)(2,1)S(1)}, bf16[2,3,8,6400]{3,2,1,0:T(8,128)(2,1)S(1)}, u32[]{:S(2)}, u32[]{:S(2)}) %collective-permute-start.10) | collective-permute-done | bytes 614432 | tf_op jit(solution)/shard_map/ppermute | solution.py:295
  113.1 3.1 %collective-permute-start.12 = (bf16[2,3,8,6400]{3,2,1,0:T(8,128)(2,1)S(1)}, bf16[2,3,8,6400]{3,2,1,0:T(8,128)(2,1)}, u32[]{:S(2)}, u32[]{:S(2)}) collective-permute-start(bf16[2,3,8,6400]{3,2,1,0:T(8,128)(2,1)S(1)} %chip.1.refs_1_), channel_id=1, source_target_pairs={{0,6},{1,7},{2,0},{3,1},{4,2},{5,3},{6,4},{7,5},{8,14},{9,15},{10,... | collective-permute-start | bytes 1843208 | tf_op jit(solution)/shard_map/ppermute | solution.py:295
  116.2 1.7 %collective-permute-done.6.others_ref.refs_3_ = bf16[2,3,8,6400]{3,2,1,0:T(8,128)(2,1)S(1)} collective-permute-done((bf16[2,3,8,6400]{3,2,1,0:T(8,128)(2,1)S(1)}, bf16[2,3,8,6400]{3,2,1,0:T(8,128)(2,1)S(1)}, u32[]{:S(2)}, u32[]{:S(2)}) %collective-permute-start.6) | collective-permute-done | bytes 614432 | tf_op jit(solution)/shard_map/ppermute | solution.py:295
  119.7 1.3 momentum_relay.1
  121.8 5.4 %all-to-all-start.2 = ((bf16[16,8,1664]{2,1,0:T(8,128)(2,1)}), bf16[16,8,1664]{2,1,0:T(8,128)(2,1)S(1)}, u32[]{:S(2)}, u32[]{:S(2)}) async-start(bf16[16,8,1664]{2,1,0:T(8,128)(2,1)} %copy-done.8), calls=%async_computation.2 | async-start | bytes 851968 | tf_op jit(solution)/shard_map/all_to_all | solution.py:298
  127.2 2.4 %collective-permute-done.12.others_ref.refs_5_ = bf16[2,3,8,6400]{3,2,1,0:T(8,128)(2,1)} collective-permute-done((bf16[2,3,8,6400]{3,2,1,0:T(8,128)(2,1)S(1)}, bf16[2,3,8,6400]{3,2,1,0:T(8,128)(2,1)}, u32[]{:S(2)}, u32[]{:S(2)}) %collective-permute-start.12) | collective-permute-done | bytes 614432 | tf_op jit(solution)/shard_map/ppermute | solution.py:295
  129.6 3.2 %collective-permute-done.11.refs_0_.refs_3_ = bf16[2,3,8,6400]{3,2,1,0:T(8,128)(2,1)} collective-permute-done((bf16[2,3,8,6400]{3,2,1,0:T(8,128)(2,1)S(1)}, bf16[2,3,8,6400]{3,2,1,0:T(8,128)(2,1)}, u32[]{:S(2)}, u32[]{:S(2)}) %collective-permute-start.11) | collective-permute-done | bytes 614432 | tf_op jit(solution)/shard_map/ppermute | solution.py:295
  132.8 1.1 onward.3.refs_7_
  134.3 8.4 %all-to-all-done.2.back_ref = bf16[16,8,1664]{2,1,0:T(8,128)(2,1)S(1)} async-done(((bf16[16,8,1664]{2,1,0:T(8,128)(2,1)}), bf16[16,8,1664]{2,1,0:T(8,128)(2,1)S(1)}, u32[]{:S(2)}, u32[]{:S(2)}) %all-to-all-start.2) | async-done | bytes 426016 | tf_op jit(solution)/shard_map/all_to_all | solution.py:298
  143.6 6.7 %collective-permute-done.14.refs_6_ = bf16[2,4,8,6400]{3,2,1,0:T(8,128)(2,1)} collective-permute-done((bf16[2,4,8,6400]{3,2,1,0:T(8,128)(2,1)}, bf16[2,4,8,6400]{3,2,1,0:T(8,128)(2,1)}, u32[]{:S(2)}, u32[]{:S(2)}) %collective-permute-start.14) | collective-permute-done | bytes 819232 | tf_op jit(solution)/shard_map/ppermute | solution.py:295
  151.4 2.9 %evaluate.2 = (bf16[2,1,64,25600]{3,2,1,0:T(8,128)(2,1)}, bf16[2,64,6400]{2,1,0:T(8,128)(2,1)S(1)}) custom-call(s32[1]{0:T(128)} %bitcast.core_ref, bf16[2,128,128]{2,1,0:T(8,128)(2,1)S(1)} %copy-done.12, bf16[2,2,8,6400]{3,2,1,0:T(8,128)(2,1)S(1)} %copy-done.10, bf16[2,3,8,6400]{3,2,1,0:T(8,128)(2,1)S(1)} %copy-done.15, ...), custom_call_target="tpu_custom_call" | custom-call | flops 419430400 | bytes 3276800 | tf_op jit(solution)/shard_map/evaluate/pallas_call | solution.py:404
  154.3 1.1 collective-permute-start.16
  155.4 3.3 %evaluate.3 = (bf16[2,1,64,25600]{3,2,1,0:T(8,128)(2,1)}, bf16[2,64,6400]{2,1,0:T(8,128)(2,1)S(1)}) custom-call(s32[1]{0:T(128)} %bitcast.core_ref, bf16[2,128,128]{2,1,0:T(8,128)(2,1)S(1)} %copy-done.12, bf16[2,2,8,6400]{3,2,1,0:T(8,128)(2,1)S(1)} %copy-done.10, bf16[2,3,8,6400]{3,2,1,0:T(8,128)(2,1)S(1)} %chip.1.refs_1_, ...), custom_call_target="tpu_custom_call", output_to_operand_aliasing={{0}: (10, {})} | custom-call | flops 419430400 | bytes 3276800 | tf_op jit(solution)/shard_map/evaluate/pallas_call | solution.py:404
  158.8 1.2 place.2.buffer_ref
  160.1 2.2 %collective-permute-done.15.piece_ref = bf16[2,64,6400]{2,1,0:T(8,128)(2,1)S(1)} collective-permute-done((bf16[2,64,6400]{2,1,0:T(8,128)(2,1)S(1)}, bf16[2,64,6400]{2,1,0:T(8,128)(2,1)S(1)}, u32[]{:S(2)}, u32[]{:S(2)}) %collective-permute-start.15) | collective-permute-done | bytes 1638432 | tf_op jit(solution)/shard_map/ppermute | solution.py:295
  162.3 1.2 place.3
  (70 shorter events, 10.6 us)
Async XLA Ops:
  5.4 11.8 %copy-start.17 = (bf16[2,1,64,128]{3,2,1,0:T(8,128)(2,1)S(1)}, bf16[2,1,64,128]{3,2,1,0:T(8,128)(2,1)}, u32[]{:S(2)}) copy-start(bf16[2,1,64,128]{3,2,1,0:T(8,128)(2,1)} %param.12) | copy-start | bytes 98308
  5.4 13.3 %copy-start.1 = (f32[1,8,25600]{2,1,0:T(8,128)S(1)}, f32[1,8,25600]{2,1,0:T(8,128)}, u32[]{:S(2)}) copy-start(f32[1,8,25600]{2,1,0:T(8,128)} %m_ref.1) | copy-start | bytes 2457604
  5.4 41.9 %all-to-all-start = ((bf16[16,3,8,1664]{3,2,1,0:T(8,128)(2,1)}), bf16[16,3,8,1664]{3,2,1,0:T(8,128)(2,1)S(1)}, u32[]{:S(2)}, u32[]{:S(2)}) async-start(bf16[16,3,8,1664]{3,2,1,0:T(8,128)(2,1)} %get-tuple-element.18), calls=%async_computation | async-start | bytes 2555904 | tf_op jit(solution)/shard_map/all_to_all | solution.py:298
  17.3 6.1 %collective-permute-start = (bf16[2,64,128]{1,2,0:T(8,128)(2,1)S(1)}, bf16[2,64,128]{1,2,0:T(8,128)(2,1)S(1)}, u32[]{:S(2)}, u32[]{:S(2)}) collective-permute-start(bf16[2,64,128]{1,2,0:T(8,128)(2,1)S(1)} %bitcast.43), channel_id=1, source_target_pairs={{0,1},{1,0},{2,3},{3,2},{4,5},{5,4},{6,7},{7,6},{8,9},{9,8},{10,11... | collective-permute-start | bytes 98312 | tf_op jit(solution)/shard_map/ppermute | solution.py:295
  18.8 1.1 copy-start.2
  19.9 1.1 copy-start.3
  23.4 24.0 %copy-start.16 = (s32[2,16]{1,0:T(2,128)S(1)}, s32[2,16]{1,0:T(2,128)}, u32[]{:S(2)}) copy-start(s32[2,16]{1,0:T(2,128)} %matching_ref.3) | copy-start | bytes 388
  24.2 55.8 %copy-start.11 = (bf16[2,128,128]{2,1,0:T(8,128)(2,1)}, bf16[2,128,128]{2,1,0:T(8,128)(2,1)S(1)}, u32[]{:S(2)}) copy-start(bf16[2,128,128]{2,1,0:T(8,128)(2,1)S(1)} %broadcast_select_fusion.tokens_ref) | copy-start | bytes 196612
  47.4 32.7 %copy-start.13 = (f32[8,25600]{1,0:T(8,128)S(1)}, f32[8,25600]{1,0:T(8,128)}, u32[]{:S(2)}) copy-start(f32[8,25600]{1,0:T(8,128)} %get-tuple-element.19.d1_ref) | copy-start | bytes 2457604
  81.3 15.3 %collective-permute-start.5 = (bf16[2,2,8,6400]{3,2,1,0:T(8,128)(2,1)S(1)}, bf16[2,2,8,6400]{3,2,1,0:T(8,128)(2,1)S(1)}, u32[]{:S(2)}, u32[]{:S(2)}) collective-permute-start(bf16[2,2,8,6400]{3,2,1,0:T(8,128)(2,1)S(1)} %get-tuple-element.21.refs_0_), channel_id=1, source_target_pairs={{0,6},{1,7},{2,0},{3,1},{4,2},{5,3},{6,4},{7,5},{8,14},{9,15},{10,... | collective-permute-start | bytes 1228808 | tf_op jit(solution)/shard_map/ppermute | solution.py:295
  84.0 12.5 %collective-permute-start.1 = (bf16[2,2,8,6400]{3,2,1,0:T(8,128)(2,1)S(1)}, bf16[2,2,8,6400]{3,2,1,0:T(8,128)(2,1)S(1)}, u32[]{:S(2)}, u32[]{:S(2)}) collective-permute-start(bf16[2,2,8,6400]{3,2,1,0:T(8,128)(2,1)S(1)} %get-tuple-element.21.refs_0_), channel_id=1, source_target_pairs={{0,2},{1,3},{2,4},{3,5},{4,6},{5,7},{6,0},{7,1},{8,10},{9,11},{10,... | collective-permute-start | bytes 1228808 | tf_op jit(solution)/shard_map/ppermute | solution.py:295
  84.8 4.9 %collective-permute-start.3 = (bf16[2,8,6400]{2,1,0:T(8,128)(2,1)S(1)}, bf16[2,8,6400]{2,1,0:T(8,128)(2,1)S(1)}, u32[]{:S(2)}, u32[]{:S(2)}) collective-permute-start(bf16[2,8,6400]{2,1,0:T(8,128)(2,1)S(1)} %get-tuple-element.23), channel_id=1, source_target_pairs={{0,8},{1,9},{2,10},{3,11},{4,12},{5,13},{6,14},{7,15},{8,0},{9,1},... | collective-permute-start | bytes 614408 | tf_op jit(solution)/shard_map/ppermute | solution.py:295
  84.8 11.7 %collective-permute-start.4 = (bf16[2,8,6400]{2,1,0:T(8,128)(2,1)S(1)}, bf16[2,8,6400]{2,1,0:T(8,128)(2,1)S(1)}, u32[]{:S(2)}, u32[]{:S(2)}) collective-permute-start(bf16[2,8,6400]{2,1,0:T(8,128)(2,1)S(1)} %get-tuple-element.22), channel_id=1, source_target_pairs={{0,9},{1,8},{2,11},{3,10},{4,13},{5,12},{6,15},{7,14},{8,1},{9,0},... | collective-permute-start | bytes 614408 | tf_op jit(solution)/shard_map/ppermute | solution.py:295
  88.9 7.6 %collective-permute-start.2 = (bf16[2,8,6400]{2,1,0:T(8,128)(2,1)S(1)}, bf16[2,8,6400]{2,1,0:T(8,128)(2,1)S(1)}, u32[]{:S(2)}, u32[]{:S(2)}) collective-permute-start(bf16[2,8,6400]{2,1,0:T(8,128)(2,1)S(1)} %get-tuple-element.22), channel_id=1, source_target_pairs={{0,1},{1,0},{2,3},{3,2},{4,5},{5,4},{6,7},{7,6},{8,9},{9,8},{10,11... | collective-permute-start | bytes 614408 | tf_op jit(solution)/shard_map/ppermute | solution.py:295
  96.6 22.3 %copy-start.14 = (bf16[2,3,8,6400]{3,2,1,0:T(8,128)(2,1)}, bf16[2,3,8,6400]{3,2,1,0:T(8,128)(2,1)S(1)}, u32[]{:S(2)}) copy-start(bf16[2,3,8,6400]{3,2,1,0:T(8,128)(2,1)S(1)} %get-tuple-element.26.refs_1_) | copy-start | bytes 1843204
  96.6 15.6 %collective-permute-start.10 = (bf16[2,3,8,6400]{3,2,1,0:T(8,128)(2,1)S(1)}, bf16[2,3,8,6400]{3,2,1,0:T(8,128)(2,1)S(1)}, u32[]{:S(2)}, u32[]{:S(2)}) collective-permute-start(bf16[2,3,8,6400]{3,2,1,0:T(8,128)(2,1)S(1)} %get-tuple-element.26.refs_1_), channel_id=1, source_target_pairs={{0,6},{1,7},{2,0},{3,1},{4,2},{5,3},{6,4},{7,5},{8,14},{9,15},{10,... | collective-permute-start | bytes 1843208 | tf_op jit(solution)/shard_map/ppermute | solution.py:295
  99.4 7.0 %collective-permute-start.8 = (bf16[2,8,6400]{2,1,0:T(8,128)(2,1)S(1)}, bf16[2,8,6400]{2,1,0:T(8,128)(2,1)S(1)}, u32[]{:S(2)}, u32[]{:S(2)}) collective-permute-start(bf16[2,8,6400]{2,1,0:T(8,128)(2,1)S(1)} %get-tuple-element.28), channel_id=1, source_target_pairs={{0,8},{1,9},{2,10},{3,11},{4,12},{5,13},{6,14},{7,15},{8,0},{9,1},... | collective-permute-start | bytes 614408 | tf_op jit(solution)/shard_map/ppermute | solution.py:295
  99.6 10.3 %collective-permute-start.9 = (bf16[2,8,6400]{2,1,0:T(8,128)(2,1)S(1)}, bf16[2,8,6400]{2,1,0:T(8,128)(2,1)S(1)}, u32[]{:S(2)}, u32[]{:S(2)}) collective-permute-start(bf16[2,8,6400]{2,1,0:T(8,128)(2,1)S(1)} %get-tuple-element.27), channel_id=1, source_target_pairs={{0,9},{1,8},{2,11},{3,10},{4,13},{5,12},{6,15},{7,14},{8,1},{9,0},... | collective-permute-start | bytes 614408 | tf_op jit(solution)/shard_map/ppermute | solution.py:295
  100.0 9.9 %collective-permute-start.7 = (bf16[2,8,6400]{2,1,0:T(8,128)(2,1)S(1)}, bf16[2,8,6400]{2,1,0:T(8,128)(2,1)S(1)}, u32[]{:S(2)}, u32[]{:S(2)}) collective-permute-start(bf16[2,8,6400]{2,1,0:T(8,128)(2,1)S(1)} %get-tuple-element.27), channel_id=1, source_target_pairs={{0,1},{1,0},{2,3},{3,2},{4,5},{5,4},{6,7},{7,6},{8,9},{9,8},{10,11... | collective-permute-start | bytes 614408 | tf_op jit(solution)/shard_map/ppermute | solution.py:295
  101.2 16.7 %collective-permute-start.6 = (bf16[2,3,8,6400]{3,2,1,0:T(8,128)(2,1)S(1)}, bf16[2,3,8,6400]{3,2,1,0:T(8,128)(2,1)S(1)}, u32[]{:S(2)}, u32[]{:S(2)}) collective-permute-start(bf16[2,3,8,6400]{3,2,1,0:T(8,128)(2,1)S(1)} %get-tuple-element.26.refs_1_), channel_id=1, source_target_pairs={{0,2},{1,3},{2,4},{3,5},{4,6},{5,7},{6,0},{7,1},{8,10},{9,11},{10,... | collective-permute-start | bytes 1843208 | tf_op jit(solution)/shard_map/ppermute | solution.py:295
  113.1 16.5 %collective-permute-start.12 = (bf16[2,3,8,6400]{3,2,1,0:T(8,128)(2,1)S(1)}, bf16[2,3,8,6400]{3,2,1,0:T(8,128)(2,1)}, u32[]{:S(2)}, u32[]{:S(2)}) collective-permute-start(bf16[2,3,8,6400]{3,2,1,0:T(8,128)(2,1)S(1)} %chip.1.refs_1_), channel_id=1, source_target_pairs={{0,6},{1,7},{2,0},{3,1},{4,2},{5,3},{6,4},{7,5},{8,14},{9,15},{10,... | collective-permute-start | bytes 1843208 | tf_op jit(solution)/shard_map/ppermute | solution.py:295
  116.2 16.6 %collective-permute-start.11 = (bf16[2,3,8,6400]{3,2,1,0:T(8,128)(2,1)S(1)}, bf16[2,3,8,6400]{3,2,1,0:T(8,128)(2,1)}, u32[]{:S(2)}, u32[]{:S(2)}) collective-permute-start(bf16[2,3,8,6400]{3,2,1,0:T(8,128)(2,1)S(1)} %chip.1.refs_1_), channel_id=1, source_target_pairs={{0,2},{1,3},{2,4},{3,5},{4,6},{5,7},{6,0},{7,1},{8,10},{9,11},{10,... | collective-permute-start | bytes 1843208 | tf_op jit(solution)/shard_map/ppermute | solution.py:295
  119.7 30.6 %collective-permute-start.14 = (bf16[2,4,8,6400]{3,2,1,0:T(8,128)(2,1)}, bf16[2,4,8,6400]{3,2,1,0:T(8,128)(2,1)}, u32[]{:S(2)}, u32[]{:S(2)}) collective-permute-start(bf16[2,4,8,6400]{3,2,1,0:T(8,128)(2,1)} %onward.2.refs_0_), channel_id=1, source_target_pairs={{0,2},{1,3},{2,4},{3,5},{4,6},{5,7},{6,0},{7,1},{8,10},{9,11},{10,... | collective-permute-start | bytes 2457608 | tf_op jit(solution)/shard_map/ppermute | solution.py:295
  121.8 20.9 %all-to-all-start.2 = ((bf16[16,8,1664]{2,1,0:T(8,128)(2,1)}), bf16[16,8,1664]{2,1,0:T(8,128)(2,1)S(1)}, u32[]{:S(2)}, u32[]{:S(2)}) async-start(bf16[16,8,1664]{2,1,0:T(8,128)(2,1)} %copy-done.8), calls=%async_computation.2 | async-start | bytes 851968 | tf_op jit(solution)/shard_map/all_to_all | solution.py:298
  133.9 21.5 %collective-permute-start.13 = (bf16[2,4,8,6400]{3,2,1,0:T(8,128)(2,1)S(1)}, bf16[2,4,8,6400]{3,2,1,0:T(8,128)(2,1)}, u32[]{:S(2)}, u32[]{:S(2)}) collective-permute-start(bf16[2,4,8,6400]{3,2,1,0:T(8,128)(2,1)S(1)} %onward.3.refs_7_), channel_id=1, source_target_pairs={{0,6},{1,7},{2,0},{3,1},{4,2},{5,3},{6,4},{7,5},{8,14},{9,15},{10,... | collective-permute-start | bytes 2457608 | tf_op jit(solution)/shard_map/ppermute | solution.py:295
  142.7 7.7 %copy-start.5 = (bf16[2,3,8,6400]{3,2,1,0:T(8,128)(2,1)S(1)}, bf16[2,3,8,6400]{3,2,1,0:T(8,128)(2,1)}, u32[]{:S(2)}) copy-start(bf16[2,3,8,6400]{3,2,1,0:T(8,128)(2,1)} %copy-done.4) | copy-start | bytes 1843204
  142.7 7.7 %copy-start.7 = (bf16[2,3,8,6400]{3,2,1,0:T(8,128)(2,1)S(1)}, bf16[2,3,8,6400]{3,2,1,0:T(8,128)(2,1)}, u32[]{:S(2)}) copy-start(bf16[2,3,8,6400]{3,2,1,0:T(8,128)(2,1)} %copy-done.6) | copy-start | bytes 1843204
  142.7 7.7 %copy-start.10 = (bf16[2,2,8,6400]{3,2,1,0:T(8,128)(2,1)S(1)}, bf16[2,2,8,6400]{3,2,1,0:T(8,128)(2,1)}, u32[]{:S(2)}) copy-start(bf16[2,2,8,6400]{3,2,1,0:T(8,128)(2,1)} %copy-done.9) | copy-start | bytes 1228804
  142.7 7.7 %copy-start.12 = (bf16[2,128,128]{2,1,0:T(8,128)(2,1)S(1)}, bf16[2,128,128]{2,1,0:T(8,128)(2,1)}, u32[]{:S(2)}) copy-start(bf16[2,128,128]{2,1,0:T(8,128)(2,1)} %copy-done.11) | copy-start | bytes 196612
  143.6 11.8 %copy-start = (f32[1,8,25600]{2,1,0:T(8,128)S(1)}, f32[1,8,25600]{2,1,0:T(8,128)}, u32[]{:S(2)}) copy-start(f32[1,8,25600]{2,1,0:T(8,128)} %momentum.1.refs_7_) | copy-start | bytes 2457604
  154.3 4.5 %collective-permute-start.16 = (bf16[2,64,6400]{2,1,0:T(8,128)(2,1)S(1)}, bf16[2,64,6400]{2,1,0:T(8,128)(2,1)S(1)}, u32[]{:S(2)}, u32[]{:S(2)}) collective-permute-start(bf16[2,64,6400]{2,1,0:T(8,128)(2,1)S(1)} %get-tuple-element.31), channel_id=1, source_target_pairs={{0,1},{1,0},{2,3},{3,2},{4,5},{5,4},{6,7},{7,6},{8,9},{9,8},{10,11... | collective-permute-start | bytes 4915208 | tf_op jit(solution)/shard_map/ppermute | solution.py:295
  158.7 3.6 %collective-permute-start.15 = (bf16[2,64,6400]{2,1,0:T(8,128)(2,1)S(1)}, bf16[2,64,6400]{2,1,0:T(8,128)(2,1)S(1)}, u32[]{:S(2)}, u32[]{:S(2)}) collective-permute-start(bf16[2,64,6400]{2,1,0:T(8,128)(2,1)S(1)} %get-tuple-element.30), channel_id=1, source_target_pairs={{0,1},{1,0},{2,3},{3,2},{4,5},{5,4},{6,7},{7,6},{8,9},{9,8},{10,11... | collective-permute-start | bytes 4915208 | tf_op jit(solution)/shard_map/ppermute | solution.py:295
  (5 other events, 4.3 us)

commit v3 on v2

--- a/solution.py
+++ b/solution.py
@@ -363,9 +363,7 @@
         10 * unit,
     )(*to_chip(kept_low, sent_low), kept_high, sent_high, own_up, own_down)
     low_up, low_down = permute(low, dy=1), permute(low, dy=-1)
-    high = call(chip_kernel, "chip", [whole] * 3 + [loose], whole, chip, 0, 6 * unit)(
-        *to_chip(kept_high, sent_high), low_down
-    )
+    high = call(chip_kernel, "chip", [whole] * 3, whole, chip, 0, 6 * unit)(*to_chip(kept_high, sent_high))
     high_down, high_up = permute(high, dy=-1), permute(high, dy=1)
     far_rows = jax.ShapeDtypeStruct((steps, 4, rows, quarter), BF16)
 
@@ -374,7 +372,7 @@
         in_specs = [whole] * 2 + [loose] * len(after)
         return call(kernel, "onward", in_specs, whole, far_rows, 0, 8 * unit)(own, others, *after)
 
-    low_onward = onward(0, own_up, low_up)
+    low_onward = onward(0, own_up, low_up, low_down)
     low_far = permute(low_onward, dy=1)
     high_onward = onward(1, own_down, high_down, high_up)
     high_far = permute(high_onward, dy=-1)

time: 164 us -> 162 us (0.988)
  no operation moved by 1% of the time
where the time goes in v3:
time: 162 us
  waiting for transfers between devices  66.6 us (41%)
  starting transfers between devices  32.9 us (20%)
  blocking collectives  31.4 us (19%)
  Pallas kernels  22.8 us (14%)
  local copies, waits for them, and re-layouts  7.04 us (4%)
    ppermute x17, waiting for transfers between devices, permute(): return lax.ppermute(value, 'fsdp', pairs)  34.3 us
    all_to_all x2, waiting for transfers between devices, relayed(): return lax.all_to_all(value, 'rep', 0, 0, tiled=True)  32.3 us
    all_to_all x1, blocking collectives, relayed(): return lax.all_to_all(value, 'rep', 0, 0, tiled=True)  31.4 us
    all_to_all x2, starting transfers between devices, relayed(): return lax.all_to_all(value, 'rep', 0, 0, tiled=True)  17.1 us
    ppermute x17, starting transfers between devices, permute(): return lax.ppermute(value, 'fsdp', pairs)  15.8 us
    pallas_call x2, Pallas kernels, evaluate(): call(kernel, 'evaluate', in_specs, [far, whole], [products, sent_products...  6.15 us
    unnamed x37, local copies, waits for them, and re-layouts  5.96 us
    pallas_call x1, Pallas kernels, shards(): call(pack_kernel, 'pack', [far] * 5, [whole] * 2, [moved, flat], 100 * un...  4.76 us
  transfers between devices with their start and end apart: 19, of which 12 were waited for; matrix products, arithmetic and copies ran while one was open for 1% of the time, Pallas kernels for 9%

profile of v3, /device:TPU:1, one launch (start us, length us, event | category | flops | bytes accessed | tf_op | source)
XLA Modules:
  0.0 161.9 jit_solution(9069821614640319343)
XLA Ops:
  0.6 4.8 %pack.1 = (bf16[16,3,8,1664]{3,2,1,0:T(8,128)(2,1)}, f32[8,25600]{1,0:T(8,128)}) custom-call(f32[1,8,25600]{2,1,0:T(8,128)} %refs_0_.1, f32[1,8,25600]{2,1,0:T(8,128)} %refs_1_.1, f32[1,8,25600]{2,1,0:T(8,128)} %m_ref.1, f32[1,8,25600]{2,1,0:T(8,128)} %v_ref.1, bf16[2,1,8,25600]{3,2,1,0:T(8,128)(2,1)} %g_ref.1), custom_call_target="tpu_custom_call" | custom-call | flops 20480000 | bytes 5324800 | tf_op jit(solution)/shard_map/pack/pallas_call | solution.py:315
  5.4 11.7 %all-to-all-start = ((bf16[16,3,8,1664]{3,2,1,0:T(8,128)(2,1)}), bf16[16,3,8,1664]{3,2,1,0:T(8,128)(2,1)S(1)}, u32[]{:S(2)}, u32[]{:S(2)}) async-start(bf16[16,3,8,1664]{3,2,1,0:T(8,128)(2,1)} %get-tuple-element.18), calls=%async_computation | async-start | bytes 2555904 | tf_op jit(solution)/shard_map/all_to_all | solution.py:298
  18.8 1.1 copy-done.2
  19.9 1.1 copy-done.3
  21.1 2.3 %second.1.d_ref.d2_ref = f32[8,25600]{1,0:T(8,128)S(1)} custom-call(f32[1,8,25600]{2,1,0:T(8,128)S(1)} %copy-done.1, f32[1,8,25600]{2,1,0:T(8,128)S(1)} %copy-done.2, bf16[2,1,8,25600]{3,2,1,0:T(8,128)(2,1)S(1)} %copy-done.3), custom_call_target="tpu_custom_call" | custom-call | flops 24576000 | bytes 2867200 | tf_op jit(solution)/shard_map/second/pallas_call | solution.py:328
  24.2 23.1 %all-to-all-done.got_ref = bf16[16,3,8,1664]{3,2,1,0:T(8,128)(2,1)S(1)} async-done(((bf16[16,3,8,1664]{3,2,1,0:T(8,128)(2,1)}), bf16[16,3,8,1664]{3,2,1,0:T(8,128)(2,1)S(1)}, u32[]{:S(2)}, u32[]{:S(2)}) %all-to-all-start) | async-done | bytes 1277984 | tf_op jit(solution)/shard_map/all_to_all | solution.py:298
  47.4 1.3 relay.1
  48.7 31.4 %all_to_all.15.back_ref = bf16[16,2,8,1664]{3,2,1,0:T(8,128)(2,1)S(1)} all-to-all(bf16[16,2,8,1664]{3,2,1,0:T(8,128)(2,1)S(1)} %relay.1), channel_id=1, replica_groups=mesh['rep'=16,'fsdp'=16] {'rep'}, dimensions={0} | all-to-all | bytes 1703936 | tf_op jit(solution)/shard_map/all_to_all | solution.py:298
  80.0 1.2 weights.1
  81.3 2.7 %collective-permute-start.5 = (bf16[2,2,8,6400]{3,2,1,0:T(8,128)(2,1)S(1)}, bf16[2,2,8,6400]{3,2,1,0:T(8,128)(2,1)S(1)}, u32[]{:S(2)}, u32[]{:S(2)}) collective-permute-start(bf16[2,2,8,6400]{3,2,1,0:T(8,128)(2,1)S(1)} %get-tuple-element.21.refs_0_), channel_id=1, source_target_pairs={{0,6},{1,7},{2,0},{3,1},{4,2},{5,3},{6,4},{7,5},{8,14},{9,15},{10,... | collective-permute-start | bytes 1228808 | tf_op jit(solution)/shard_map/ppermute | solution.py:295
  84.8 4.2 %collective-permute-start.4 = (bf16[2,8,6400]{2,1,0:T(8,128)(2,1)S(1)}, bf16[2,8,6400]{2,1,0:T(8,128)(2,1)S(1)}, u32[]{:S(2)}, u32[]{:S(2)}) collective-permute-start(bf16[2,8,6400]{2,1,0:T(8,128)(2,1)S(1)} %get-tuple-element.22), channel_id=1, source_target_pairs={{0,9},{1,8},{2,11},{3,10},{4,13},{5,12},{6,15},{7,14},{8,1},{9,0},... | collective-permute-start | bytes 614408 | tf_op jit(solution)/shard_map/ppermute | solution.py:295
  89.7 6.8 %collective-permute-done.4.refs_2_ = bf16[2,8,6400]{2,1,0:T(8,128)(2,1)S(1)} collective-permute-done((bf16[2,8,6400]{2,1,0:T(8,128)(2,1)S(1)}, bf16[2,8,6400]{2,1,0:T(8,128)(2,1)S(1)}, u32[]{:S(2)}, u32[]{:S(2)}) %collective-permute-start.4) | collective-permute-done | bytes 204832 | tf_op jit(solution)/shard_map/ppermute | solution.py:295
  96.7 2.2 %collective-permute-start.10 = (bf16[2,8,6400]{2,1,0:T(8,128)(2,1)S(1)}, bf16[2,8,6400]{2,1,0:T(8,128)(2,1)S(1)}, u32[]{:S(2)}, u32[]{:S(2)}) collective-permute-start(bf16[2,8,6400]{2,1,0:T(8,128)(2,1)S(1)} %get-tuple-element.27), channel_id=1, source_target_pairs={{0,9},{1,8},{2,11},{3,10},{4,13},{5,12},{6,15},{7,14},{8,1},{9,0},... | collective-permute-start | bytes 614408 | tf_op jit(solution)/shard_map/ppermute | solution.py:295
  98.9 2.3 %collective-permute-start.7 = (bf16[2,3,8,6400]{3,2,1,0:T(8,128)(2,1)S(1)}, bf16[2,3,8,6400]{3,2,1,0:T(8,128)(2,1)S(1)}, u32[]{:S(2)}, u32[]{:S(2)}) collective-permute-start(bf16[2,3,8,6400]{3,2,1,0:T(8,128)(2,1)S(1)} %get-tuple-element.26.refs_1_), channel_id=1, source_target_pairs={{0,6},{1,7},{2,0},{3,1},{4,2},{5,3},{6,4},{7,5},{8,14},{9,15},{10,... | collective-permute-start | bytes 1843208 | tf_op jit(solution)/shard_map/ppermute | solution.py:295
  101.2 1.6 collective-permute-done.9.refs_1_
  102.8 5.4 %collective-permute-done.10.refs_2_ = bf16[2,8,6400]{2,1,0:T(8,128)(2,1)S(1)} collective-permute-done((bf16[2,8,6400]{2,1,0:T(8,128)(2,1)S(1)}, bf16[2,8,6400]{2,1,0:T(8,128)(2,1)S(1)}, u32[]{:S(2)}, u32[]{:S(2)}) %collective-permute-start.10) | collective-permute-done | bytes 204832 | tf_op jit(solution)/shard_map/ppermute | solution.py:295
  108.3 1.2 collective-permute-start.12
  109.8 4.7 %collective-permute-done.7.refs_0_.refs_5_ = bf16[2,3,8,6400]{3,2,1,0:T(8,128)(2,1)S(1)} collective-permute-done((bf16[2,3,8,6400]{3,2,1,0:T(8,128)(2,1)S(1)}, bf16[2,3,8,6400]{3,2,1,0:T(8,128)(2,1)S(1)}, u32[]{:S(2)}, u32[]{:S(2)}) %collective-permute-start.7) | collective-permute-done | bytes 614432 | tf_op jit(solution)/shard_map/ppermute | solution.py:295
  114.5 3.1 %collective-permute-done.6.others_ref.refs_3_ = bf16[2,3,8,6400]{3,2,1,0:T(8,128)(2,1)S(1)} collective-permute-done((bf16[2,3,8,6400]{3,2,1,0:T(8,128)(2,1)S(1)}, bf16[2,3,8,6400]{3,2,1,0:T(8,128)(2,1)S(1)}, u32[]{:S(2)}, u32[]{:S(2)}) %collective-permute-start.6) | collective-permute-done | bytes 614432 | tf_op jit(solution)/shard_map/ppermute | solution.py:295
  119.6 1.3 momentum_relay.1
  121.6 5.4 %all-to-all-start.2 = ((bf16[16,8,1664]{2,1,0:T(8,128)(2,1)}), bf16[16,8,1664]{2,1,0:T(8,128)(2,1)S(1)}, u32[]{:S(2)}, u32[]{:S(2)}) async-start(bf16[16,8,1664]{2,1,0:T(8,128)(2,1)} %copy-done.8), calls=%async_computation.2 | async-start | bytes 851968 | tf_op jit(solution)/shard_map/all_to_all | solution.py:298
  127.7 3.2 %collective-permute-done.11.refs_0_.refs_3_ = bf16[2,3,8,6400]{3,2,1,0:T(8,128)(2,1)} collective-permute-done((bf16[2,3,8,6400]{3,2,1,0:T(8,128)(2,1)S(1)}, bf16[2,3,8,6400]{3,2,1,0:T(8,128)(2,1)}, u32[]{:S(2)}, u32[]{:S(2)}) %collective-permute-start.11) | collective-permute-done | bytes 614432 | tf_op jit(solution)/shard_map/ppermute | solution.py:295
  130.9 1.1 onward.3.refs_7_
  132.4 9.1 %all-to-all-done.2.back_ref = bf16[16,8,1664]{2,1,0:T(8,128)(2,1)S(1)} async-done(((bf16[16,8,1664]{2,1,0:T(8,128)(2,1)}), bf16[16,8,1664]{2,1,0:T(8,128)(2,1)S(1)}, u32[]{:S(2)}, u32[]{:S(2)}) %all-to-all-start.2) | async-done | bytes 426016 | tf_op jit(solution)/shard_map/all_to_all | solution.py:298
  142.5 5.9 %collective-permute-done.14.refs_6_ = bf16[2,4,8,6400]{3,2,1,0:T(8,128)(2,1)} collective-permute-done((bf16[2,4,8,6400]{3,2,1,0:T(8,128)(2,1)}, bf16[2,4,8,6400]{3,2,1,0:T(8,128)(2,1)}, u32[]{:S(2)}, u32[]{:S(2)}) %collective-permute-start.14) | collective-permute-done | bytes 819232 | tf_op jit(solution)/shard_map/ppermute | solution.py:295
  148.5 1.1 copy-done.15
  149.5 2.9 %evaluate.2 = (bf16[2,1,64,25600]{3,2,1,0:T(8,128)(2,1)}, bf16[2,64,6400]{2,1,0:T(8,128)(2,1)S(1)}) custom-call(s32[1]{0:T(128)} %bitcast.core_ref, bf16[2,128,128]{2,1,0:T(8,128)(2,1)S(1)} %copy-done.12, bf16[2,2,8,6400]{3,2,1,0:T(8,128)(2,1)S(1)} %copy-done.10, bf16[2,3,8,6400]{3,2,1,0:T(8,128)(2,1)S(1)} %copy-done.15, ...), custom_call_target="tpu_custom_call" | custom-call | flops 419430400 | bytes 3276800 | tf_op jit(solution)/shard_map/evaluate/pallas_call | solution.py:402
  152.4 1.2 collective-permute-start.16
  153.6 3.3 %evaluate.3 = (bf16[2,1,64,25600]{3,2,1,0:T(8,128)(2,1)}, bf16[2,64,6400]{2,1,0:T(8,128)(2,1)S(1)}) custom-call(s32[1]{0:T(128)} %bitcast.core_ref, bf16[2,128,128]{2,1,0:T(8,128)(2,1)S(1)} %copy-done.12, bf16[2,2,8,6400]{3,2,1,0:T(8,128)(2,1)S(1)} %copy-done.10, bf16[2,3,8,6400]{3,2,1,0:T(8,128)(2,1)S(1)} %chip.1.refs_1_, ...), custom_call_target="tpu_custom_call", output_to_operand_aliasing={{0}: (10, {})} | custom-call | flops 419430400 | bytes 3276800 | tf_op jit(solution)/shard_map/evaluate/pallas_call | solution.py:402
  157.0 1.2 place.2.buffer_ref
  158.3 2.2 %collective-permute-done.15.piece_ref = bf16[2,64,6400]{2,1,0:T(8,128)(2,1)S(1)} collective-permute-done((bf16[2,64,6400]{2,1,0:T(8,128)(2,1)S(1)}, bf16[2,64,6400]{2,1,0:T(8,128)(2,1)S(1)}, u32[]{:S(2)}, u32[]{:S(2)}) %collective-permute-start.15) | collective-permute-done | bytes 1638432 | tf_op jit(solution)/shard_map/ppermute | solution.py:295
  160.5 1.2 place.3
  (70 shorter events, 9.3 us)
Async XLA Ops:
  5.4 11.8 %copy-start.17 = (bf16[2,1,64,128]{3,2,1,0:T(8,128)(2,1)S(1)}, bf16[2,1,64,128]{3,2,1,0:T(8,128)(2,1)}, u32[]{:S(2)}) copy-start(bf16[2,1,64,128]{3,2,1,0:T(8,128)(2,1)} %param.12) | copy-start | bytes 98308
  5.4 13.3 %copy-start.1 = (f32[1,8,25600]{2,1,0:T(8,128)S(1)}, f32[1,8,25600]{2,1,0:T(8,128)}, u32[]{:S(2)}) copy-start(f32[1,8,25600]{2,1,0:T(8,128)} %m_ref.1) | copy-start | bytes 2457604
  5.4 41.9 %all-to-all-start = ((bf16[16,3,8,1664]{3,2,1,0:T(8,128)(2,1)}), bf16[16,3,8,1664]{3,2,1,0:T(8,128)(2,1)S(1)}, u32[]{:S(2)}, u32[]{:S(2)}) async-start(bf16[16,3,8,1664]{3,2,1,0:T(8,128)(2,1)} %get-tuple-element.18), calls=%async_computation | async-start | bytes 2555904 | tf_op jit(solution)/shard_map/all_to_all | solution.py:298
  17.3 6.1 %collective-permute-start = (bf16[2,64,128]{1,2,0:T(8,128)(2,1)S(1)}, bf16[2,64,128]{1,2,0:T(8,128)(2,1)S(1)}, u32[]{:S(2)}, u32[]{:S(2)}) collective-permute-start(bf16[2,64,128]{1,2,0:T(8,128)(2,1)S(1)} %bitcast.43), channel_id=1, source_target_pairs={{0,1},{1,0},{2,3},{3,2},{4,5},{5,4},{6,7},{7,6},{8,9},{9,8},{10,11... | collective-permute-start | bytes 98312 | tf_op jit(solution)/shard_map/ppermute | solution.py:295
  18.8 1.1 copy-start.2
  19.9 1.1 copy-start.3
  23.4 24.0 %copy-start.16 = (s32[2,16]{1,0:T(2,128)S(1)}, s32[2,16]{1,0:T(2,128)}, u32[]{:S(2)}) copy-start(s32[2,16]{1,0:T(2,128)} %matching_ref.3) | copy-start | bytes 388
  24.2 55.8 %copy-start.11 = (bf16[2,128,128]{2,1,0:T(8,128)(2,1)}, bf16[2,128,128]{2,1,0:T(8,128)(2,1)S(1)}, u32[]{:S(2)}) copy-start(bf16[2,128,128]{2,1,0:T(8,128)(2,1)S(1)} %broadcast_select_fusion.tokens_ref) | copy-start | bytes 196612
  47.4 32.7 %copy-start.13 = (f32[8,25600]{1,0:T(8,128)S(1)}, f32[8,25600]{1,0:T(8,128)}, u32[]{:S(2)}) copy-start(f32[8,25600]{1,0:T(8,128)} %get-tuple-element.19.d1_ref) | copy-start | bytes 2457604
  81.3 15.3 %collective-permute-start.5 = (bf16[2,2,8,6400]{3,2,1,0:T(8,128)(2,1)S(1)}, bf16[2,2,8,6400]{3,2,1,0:T(8,128)(2,1)S(1)}, u32[]{:S(2)}, u32[]{:S(2)}) collective-permute-start(bf16[2,2,8,6400]{3,2,1,0:T(8,128)(2,1)S(1)} %get-tuple-element.21.refs_0_), channel_id=1, source_target_pairs={{0,6},{1,7},{2,0},{3,1},{4,2},{5,3},{6,4},{7,5},{8,14},{9,15},{10,... | collective-permute-start | bytes 1228808 | tf_op jit(solution)/shard_map/ppermute | solution.py:295
  84.0 12.5 %collective-permute-start.1 = (bf16[2,2,8,6400]{3,2,1,0:T(8,128)(2,1)S(1)}, bf16[2,2,8,6400]{3,2,1,0:T(8,128)(2,1)S(1)}, u32[]{:S(2)}, u32[]{:S(2)}) collective-permute-start(bf16[2,2,8,6400]{3,2,1,0:T(8,128)(2,1)S(1)} %get-tuple-element.21.refs_0_), channel_id=1, source_target_pairs={{0,2},{1,3},{2,4},{3,5},{4,6},{5,7},{6,0},{7,1},{8,10},{9,11},{10,... | collective-permute-start | bytes 1228808 | tf_op jit(solution)/shard_map/ppermute | solution.py:295
  84.8 4.9 %collective-permute-start.3 = (bf16[2,8,6400]{2,1,0:T(8,128)(2,1)S(1)}, bf16[2,8,6400]{2,1,0:T(8,128)(2,1)S(1)}, u32[]{:S(2)}, u32[]{:S(2)}) collective-permute-start(bf16[2,8,6400]{2,1,0:T(8,128)(2,1)S(1)} %get-tuple-element.23), channel_id=1, source_target_pairs={{0,8},{1,9},{2,10},{3,11},{4,12},{5,13},{6,14},{7,15},{8,0},{9,1},... | collective-permute-start | bytes 614408 | tf_op jit(solution)/shard_map/ppermute | solution.py:295
  84.8 11.7 %collective-permute-start.4 = (bf16[2,8,6400]{2,1,0:T(8,128)(2,1)S(1)}, bf16[2,8,6400]{2,1,0:T(8,128)(2,1)S(1)}, u32[]{:S(2)}, u32[]{:S(2)}) collective-permute-start(bf16[2,8,6400]{2,1,0:T(8,128)(2,1)S(1)} %get-tuple-element.22), channel_id=1, source_target_pairs={{0,9},{1,8},{2,11},{3,10},{4,13},{5,12},{6,15},{7,14},{8,1},{9,0},... | collective-permute-start | bytes 614408 | tf_op jit(solution)/shard_map/ppermute | solution.py:295
  88.9 7.6 %collective-permute-start.2 = (bf16[2,8,6400]{2,1,0:T(8,128)(2,1)S(1)}, bf16[2,8,6400]{2,1,0:T(8,128)(2,1)S(1)}, u32[]{:S(2)}, u32[]{:S(2)}) collective-permute-start(bf16[2,8,6400]{2,1,0:T(8,128)(2,1)S(1)} %get-tuple-element.22), channel_id=1, source_target_pairs={{0,1},{1,0},{2,3},{3,2},{4,5},{5,4},{6,7},{7,6},{8,9},{9,8},{10,11... | collective-permute-start | bytes 614408 | tf_op jit(solution)/shard_map/ppermute | solution.py:295
  96.6 22.0 %copy-start.14 = (bf16[2,3,8,6400]{3,2,1,0:T(8,128)(2,1)}, bf16[2,3,8,6400]{3,2,1,0:T(8,128)(2,1)S(1)}, u32[]{:S(2)}) copy-start(bf16[2,3,8,6400]{3,2,1,0:T(8,128)(2,1)S(1)} %get-tuple-element.26.refs_1_) | copy-start | bytes 1843204
  96.6 6.2 %collective-permute-start.9 = (bf16[2,8,6400]{2,1,0:T(8,128)(2,1)S(1)}, bf16[2,8,6400]{2,1,0:T(8,128)(2,1)S(1)}, u32[]{:S(2)}, u32[]{:S(2)}) collective-permute-start(bf16[2,8,6400]{2,1,0:T(8,128)(2,1)S(1)} %get-tuple-element.28), channel_id=1, source_target_pairs={{0,8},{1,9},{2,10},{3,11},{4,12},{5,13},{6,14},{7,15},{8,0},{9,1},... | collective-permute-start | bytes 614408 | tf_op jit(solution)/shard_map/ppermute | solution.py:295
  96.7 11.5 %collective-permute-start.10 = (bf16[2,8,6400]{2,1,0:T(8,128)(2,1)S(1)}, bf16[2,8,6400]{2,1,0:T(8,128)(2,1)S(1)}, u32[]{:S(2)}, u32[]{:S(2)}) collective-permute-start(bf16[2,8,6400]{2,1,0:T(8,128)(2,1)S(1)} %get-tuple-element.27), channel_id=1, source_target_pairs={{0,9},{1,8},{2,11},{3,10},{4,13},{5,12},{6,15},{7,14},{8,1},{9,0},... | collective-permute-start | bytes 614408 | tf_op jit(solution)/shard_map/ppermute | solution.py:295
  98.9 9.3 %collective-permute-start.8 = (bf16[2,8,6400]{2,1,0:T(8,128)(2,1)S(1)}, bf16[2,8,6400]{2,1,0:T(8,128)(2,1)S(1)}, u32[]{:S(2)}, u32[]{:S(2)}) collective-permute-start(bf16[2,8,6400]{2,1,0:T(8,128)(2,1)S(1)} %get-tuple-element.27), channel_id=1, source_target_pairs={{0,1},{1,0},{2,3},{3,2},{4,5},{5,4},{6,7},{7,6},{8,9},{9,8},{10,11... | collective-permute-start | bytes 614408 | tf_op jit(solution)/shard_map/ppermute | solution.py:295
  98.9 15.6 %collective-permute-start.7 = (bf16[2,3,8,6400]{3,2,1,0:T(8,128)(2,1)S(1)}, bf16[2,3,8,6400]{3,2,1,0:T(8,128)(2,1)S(1)}, u32[]{:S(2)}, u32[]{:S(2)}) collective-permute-start(bf16[2,3,8,6400]{3,2,1,0:T(8,128)(2,1)S(1)} %get-tuple-element.26.refs_1_), channel_id=1, source_target_pairs={{0,6},{1,7},{2,0},{3,1},{4,2},{5,3},{6,4},{7,5},{8,14},{9,15},{10,... | collective-permute-start | bytes 1843208 | tf_op jit(solution)/shard_map/ppermute | solution.py:295
  101.2 16.4 %collective-permute-start.6 = (bf16[2,3,8,6400]{3,2,1,0:T(8,128)(2,1)S(1)}, bf16[2,3,8,6400]{3,2,1,0:T(8,128)(2,1)S(1)}, u32[]{:S(2)}, u32[]{:S(2)}) collective-permute-start(bf16[2,3,8,6400]{3,2,1,0:T(8,128)(2,1)S(1)} %get-tuple-element.26.refs_1_), channel_id=1, source_target_pairs={{0,2},{1,3},{2,4},{3,5},{4,6},{5,7},{6,0},{7,1},{8,10},{9,11},{10,... | collective-permute-start | bytes 1843208 | tf_op jit(solution)/shard_map/ppermute | solution.py:295
  108.3 19.4 %collective-permute-start.12 = (bf16[2,3,8,6400]{3,2,1,0:T(8,128)(2,1)S(1)}, bf16[2,3,8,6400]{3,2,1,0:T(8,128)(2,1)}, u32[]{:S(2)}, u32[]{:S(2)}) collective-permute-start(bf16[2,3,8,6400]{3,2,1,0:T(8,128)(2,1)S(1)} %chip.1.refs_1_), channel_id=1, source_target_pairs={{0,6},{1,7},{2,0},{3,1},{4,2},{5,3},{6,4},{7,5},{8,14},{9,15},{10,... | collective-permute-start | bytes 1843208 | tf_op jit(solution)/shard_map/ppermute | solution.py:295
  109.4 21.4 %collective-permute-start.11 = (bf16[2,3,8,6400]{3,2,1,0:T(8,128)(2,1)S(1)}, bf16[2,3,8,6400]{3,2,1,0:T(8,128)(2,1)}, u32[]{:S(2)}, u32[]{:S(2)}) collective-permute-start(bf16[2,3,8,6400]{3,2,1,0:T(8,128)(2,1)S(1)} %chip.1.refs_1_), channel_id=1, source_target_pairs={{0,2},{1,3},{2,4},{3,5},{4,6},{5,7},{6,0},{7,1},{8,10},{9,11},{10,... | collective-permute-start | bytes 1843208 | tf_op jit(solution)/shard_map/ppermute | solution.py:295
  119.6 28.9 %collective-permute-start.14 = (bf16[2,4,8,6400]{3,2,1,0:T(8,128)(2,1)}, bf16[2,4,8,6400]{3,2,1,0:T(8,128)(2,1)}, u32[]{:S(2)}, u32[]{:S(2)}) collective-permute-start(bf16[2,4,8,6400]{3,2,1,0:T(8,128)(2,1)} %onward.2.refs_0_), channel_id=1, source_target_pairs={{0,2},{1,3},{2,4},{3,5},{4,6},{5,7},{6,0},{7,1},{8,10},{9,11},{10,... | collective-permute-start | bytes 2457608 | tf_op jit(solution)/shard_map/ppermute | solution.py:295
  121.6 19.9 %all-to-all-start.2 = ((bf16[16,8,1664]{2,1,0:T(8,128)(2,1)}), bf16[16,8,1664]{2,1,0:T(8,128)(2,1)S(1)}, u32[]{:S(2)}, u32[]{:S(2)}) async-start(bf16[16,8,1664]{2,1,0:T(8,128)(2,1)} %copy-done.8), calls=%async_computation.2 | async-start | bytes 851968 | tf_op jit(solution)/shard_map/all_to_all | solution.py:298
  132.0 21.6 %collective-permute-start.13 = (bf16[2,4,8,6400]{3,2,1,0:T(8,128)(2,1)S(1)}, bf16[2,4,8,6400]{3,2,1,0:T(8,128)(2,1)}, u32[]{:S(2)}, u32[]{:S(2)}) collective-permute-start(bf16[2,4,8,6400]{3,2,1,0:T(8,128)(2,1)S(1)} %onward.3.refs_7_), channel_id=1, source_target_pairs={{0,6},{1,7},{2,0},{3,1},{4,2},{5,3},{6,4},{7,5},{8,14},{9,15},{10,... | collective-permute-start | bytes 2457608 | tf_op jit(solution)/shard_map/ppermute | solution.py:295
  141.6 6.9 %copy-start.5 = (bf16[2,3,8,6400]{3,2,1,0:T(8,128)(2,1)S(1)}, bf16[2,3,8,6400]{3,2,1,0:T(8,128)(2,1)}, u32[]{:S(2)}) copy-start(bf16[2,3,8,6400]{3,2,1,0:T(8,128)(2,1)} %copy-done.4) | copy-start | bytes 1843204
  141.6 6.9 %copy-start.7 = (bf16[2,3,8,6400]{3,2,1,0:T(8,128)(2,1)S(1)}, bf16[2,3,8,6400]{3,2,1,0:T(8,128)(2,1)}, u32[]{:S(2)}) copy-start(bf16[2,3,8,6400]{3,2,1,0:T(8,128)(2,1)} %copy-done.6) | copy-start | bytes 1843204
  141.6 6.9 %copy-start.10 = (bf16[2,2,8,6400]{3,2,1,0:T(8,128)(2,1)S(1)}, bf16[2,2,8,6400]{3,2,1,0:T(8,128)(2,1)}, u32[]{:S(2)}) copy-start(bf16[2,2,8,6400]{3,2,1,0:T(8,128)(2,1)} %copy-done.9) | copy-start | bytes 1228804
  141.6 6.9 %copy-start.12 = (bf16[2,128,128]{2,1,0:T(8,128)(2,1)S(1)}, bf16[2,128,128]{2,1,0:T(8,128)(2,1)}, u32[]{:S(2)}) copy-start(bf16[2,128,128]{2,1,0:T(8,128)(2,1)} %copy-done.11) | copy-start | bytes 196612
  142.5 11.1 %copy-start = (f32[1,8,25600]{2,1,0:T(8,128)S(1)}, f32[1,8,25600]{2,1,0:T(8,128)}, u32[]{:S(2)}) copy-start(f32[1,8,25600]{2,1,0:T(8,128)} %momentum.1.refs_7_) | copy-start | bytes 2457604
  152.4 4.6 %collective-permute-start.16 = (bf16[2,64,6400]{2,1,0:T(8,128)(2,1)S(1)}, bf16[2,64,6400]{2,1,0:T(8,128)(2,1)S(1)}, u32[]{:S(2)}, u32[]{:S(2)}) collective-permute-start(bf16[2,64,6400]{2,1,0:T(8,128)(2,1)S(1)} %get-tuple-element.31), channel_id=1, source_target_pairs={{0,1},{1,0},{2,3},{3,2},{4,5},{5,4},{6,7},{7,6},{8,9},{9,8},{10,11... | collective-permute-start | bytes 4915208 | tf_op jit(solution)/shard_map/ppermute | solution.py:295
  156.9 3.6 %collective-permute-start.15 = (bf16[2,64,6400]{2,1,0:T(8,128)(2,1)S(1)}, bf16[2,64,6400]{2,1,0:T(8,128)(2,1)S(1)}, u32[]{:S(2)}, u32[]{:S(2)}) collective-permute-start(bf16[2,64,6400]{2,1,0:T(8,128)(2,1)S(1)} %get-tuple-element.30), channel_id=1, source_target_pairs={{0,1},{1,0},{2,3},{3,2},{4,5},{5,4},{6,7},{7,6},{8,9},{9,8},{10,11... | collective-permute-start | bytes 4915208 | tf_op jit(solution)/shard_map/ppermute | solution.py:295
  (5 other events, 4.5 us)
